TPU v7x, 32 devices: a whole 2x2x4 slice. The times are simulated.
32 devices in a mesh: grp: 2 (over x), ka: 8 (over z, y), pb: 2 (over core).
Axes of the slice: x: 2, y: 2, z: 4, core: 2. Of those that a mesh axis runs over, the one named last changes fastest.
Arguments:
- momentum_mesh_positions: int32 [3, 8192], P(None, 'ka'), may hold values from 0 to 99
- bravais_translation_list: int32 [512, 3], replicated, may hold values from -4 to 4
- localized_matrix_element_table: bfloat16 [32, 512, 768], P(('grp', 'pb'), 'ka'), parts along dimension 0, may hold values from -0.25 to 0.25
- unitary_band_mixer: bfloat16 [64, 16384], P(None, ('grp', 'ka')), parts along dimension 1, may hold values from -2 to 2
- quasiparticle_level_offsets: bfloat16 [8, 16384], P(None, ('grp', 'ka')), parts along dimension 1, may hold values from -0.3 to 0.3
- displaced_momentum_slot: int32 [32, 8192], P(('grp', 'pb'), 'ka'), parts along dimension 0, may hold values from 0 to 8191, as said below
- vibration_mode_pulsations: bfloat16 [32, 12], P(('grp', 'pb')), parts along dimension 0, may hold values from 0.019897461 to 0.079589844
- occupied_band_tally: int32 [16], P(('grp', 'ka')), parts along dimension 0, may hold values from 1 to 8
- heat_bath_scale: float32 [2], P('grp'), parts along dimension 0, may hold values from 0.02 to 0.06
Outputs:
- self_energy: float32 [8, 16384], P(None, ('grp', 'ka')), parts along dimension 1
- linewidth: float32 [32, 12], P(('grp', 'pb')), parts along dimension 0
There are 2 independent parts, one for each index of `grp`. A program takes and returns all parts, laid end to end along the dimension named above; an argument that names none is the same for every part. Nothing has to cross between parts.
Inputs may be any that keep to these rules, and one draw needn't show every extreme that they name: For each q, displaced_momentum_slot[q, k] = (k + s_q) mod 8192 with one shift s_q for that q.
All inputs are finite; a program needn't handle non-finite values.
Results may differ from a plain program's by a relative error of at most 0.0022.
Values may be sent and summed in bfloat16 or wider, within the bound.
A program may use at most 128 MiB of HBM per device.

v0:
```python
import math

import jax
import jax.numpy as jnp
from jax import lax
from jax.sharding import PartitionSpec as P

NB = 8
NM = 12


ETA = 0.05


def phases_by_cell(kpoints_own, cell_rows):
    product = (
        cell_rows[:, 0][:, None] * kpoints_own[0][None, :]
        + cell_rows[:, 1][:, None] * kpoints_own[1][None, :]
        + cell_rows[:, 2][:, None] * kpoints_own[2][None, :]
    )
    product = product % 100
    return jnp.cos(product.astype(jnp.float32) * (2.0 * math.pi / 100.0)).astype(jnp.bfloat16)


def lorentz(value):
    return ETA / math.pi / (value * value + ETA * ETA)


def fold_rows(kpoints_own, bravais_translation_list, portion):
    phase_rows = phases_by_cell(kpoints_own, bravais_translation_list)
    return jnp.einsum("rk,qrf->qfk", phase_rows, portion, preferred_element_type=jnp.float32)


def sweep_q(
    interp_all,
    kq_rows_all,
    freq_all,
    local_mixer,
    en_own,
    eig_all,
    en_all,
    window_top,
    occupation_multiplier,
):
    row_count = local_mixer.shape[1]
    u_here = local_mixer.astype(jnp.float32).reshape(NB, NB, row_count)
    e_here = en_own.astype(jnp.float32)
    fermi_here = 1.0 / (1.0 + jnp.exp(e_here / occupation_multiplier))
    band_mask = jnp.broadcast_to(
        (jnp.arange(NB, dtype=jnp.int32) < window_top).astype(jnp.float32)[:, None], (NB, row_count)
    )

    def advance(running, inputs):
        interp, kq_rows, mode_raw = inputs
        mode_freq = mode_raw.astype(jnp.float32)
        coupling = interp.astype(jnp.float32).reshape(NM, NB, NB, row_count)
        u_far = jnp.take(eig_all, kq_rows, axis=1).astype(jnp.float32).reshape(NB, NB, row_count)
        e_far = jnp.take(en_all, kq_rows, axis=1).astype(jnp.float32)
        inner = coupling[:, :, 0][:, :, None, :] * u_here[0][None, None, :, :]
        for index_b in range(1, NB):
            inner = (
                inner + coupling[:, :, index_b][:, :, None, :] * u_here[index_b][None, None, :, :]
            )
        inner = inner.astype(jnp.bfloat16).astype(jnp.float32)
        rotated = u_far[0][None, :, None, :] * inner[:, 0][:, None, :, :]
        for index_a in range(1, NB):
            rotated = rotated + u_far[index_a][None, :, None, :] * inner[:, index_a][:, None, :, :]
        squared = rotated * rotated
        fermi_far = 1.0 / (1.0 + jnp.exp(e_far / occupation_multiplier))
        bose = 1.0 / (jnp.exp(mode_freq / occupation_multiplier) - 1.0)
        energy_gap = e_here[None, :, :] - e_far[:, None, :]
        mode_term = mode_freq[:, None, None, None]
        plus = lorentz(energy_gap[None] + mode_term)
        minus = lorentz(energy_gap[None] - mode_term)
        bose_term = bose[:, None, None, None]
        fermi_m = fermi_far[None, :, None, :]
        kpoint_weight = (bose_term + fermi_m) * plus + (bose_term + 1.0 - fermi_m) * minus
        self_term = jnp.sum(squared * kpoint_weight, axis=(0, 1))
        flow = band_mask[None, None] * (fermi_here[None, None] - fermi_m) * plus
        width_term = 2.0 * math.pi * mode_freq * jnp.sum(squared * flow, axis=(1, 2, 3))
        return (running + self_term, width_term)

    running, widths = lax.scan(
        advance, jnp.zeros((NB, row_count), jnp.float32), (interp_all, kq_rows_all, freq_all)
    )
    return (band_mask * running, widths)


def on_device(
    momentum_mesh_positions,
    bravais_translation_list,
    localized_matrix_element_table,
    unitary_band_mixer,
    quasiparticle_level_offsets,
    displaced_momentum_slot,
    vibration_mode_pulsations,
    occupied_band_tally,
    heat_bath_scale,
):
    kcount = momentum_mesh_positions.shape[1]
    q_local = localized_matrix_element_table.shape[0]
    occupation_multiplier = heat_bath_scale[0]
    window_top = occupied_band_tally[0]
    q_total = q_local * lax.axis_size("pb")
    k_total = kcount * lax.axis_size("ka")
    eig_all, en_all = (
        lax.all_gather(unitary_band_mixer, "ka", axis=1, tiled=True),
        lax.all_gather(quasiparticle_level_offsets, "ka", axis=1, tiled=True),
    )
    coupling_all, freq_all = (
        lax.all_gather(localized_matrix_element_table, "pb", axis=0, tiled=True),
        lax.all_gather(vibration_mode_pulsations, "pb", axis=0, tiled=True),
    )
    kq_all = lax.all_gather(displaced_momentum_slot, "pb", axis=0, tiled=True)
    own_rows = kcount // lax.axis_size("pb")
    offset = lax.axis_index("pb") * own_rows
    kpoints_own = lax.dynamic_slice_in_dim(momentum_mesh_positions, offset, own_rows, 1)
    local_mixer = lax.dynamic_slice_in_dim(unitary_band_mixer, offset, own_rows, 1)
    en_own = lax.dynamic_slice_in_dim(quasiparticle_level_offsets, offset, own_rows, 1)
    kq_own = lax.dynamic_slice_in_dim(kq_all, offset, own_rows, 1)
    interp_all = fold_rows(
        kpoints_own,
        bravais_translation_list,
        lax.all_gather(coupling_all, "ka", axis=1, tiled=True),
    )
    running, widths = sweep_q(
        interp_all.astype(jnp.bfloat16),
        kq_own,
        freq_all,
        local_mixer,
        en_own,
        eig_all,
        en_all,
        window_top,
        occupation_multiplier,
    )
    part_sigma = running / (q_total * NM)
    self_energy = lax.all_gather(part_sigma, "pb", axis=1, tiled=True)
    widths = lax.psum(widths, ("ka", "pb"))
    linewidth = (
        lax.dynamic_slice_in_dim(widths, lax.axis_index("pb") * q_local, q_local, 0) / k_total
    )
    return (self_energy, linewidth)


def solution(mesh):
    return jax.shard_map(
        on_device,
        mesh=mesh,
        in_specs=(
            P(None, "ka"),
            P(),
            P(("grp", "pb"), "ka", None),
            P(None, ("grp", "ka")),
            P(None, ("grp", "ka")),
            P(("grp", "pb"), "ka"),
            P(("grp", "pb"), None),
            P(("grp", "ka")),
            P("grp"),
        ),
        out_specs=(P(None, ("grp", "ka")), P(("grp", "pb"), None)),
        check_vma=False,
    )
```

profile of v0, /device:TPU:0, one launch (start us, length us, event | category | flops | bytes accessed | tf_op | source)
XLA Modules:
  0.0 736.6 jit_solution(7076118568688248529)
XLA Ops:
  8.0 14.1 %all-gather.6.cloned.1.call-done = bf16[16,64,768]{2,1,0:T(8,128)(2,1)} async-done(((bf16[8,64,768]{2,1,0:T(8,128)(2,1)}), bf16[16,64,768]{2,1,0:T(8,128)(2,1)}) %all-gather.6.cloned.1.call-update) | async-done | bytes 1572880 | tf_op jit(solution)/shard_map/all_gather | solution.py:111
  23.1 1.9 all_gather.21
  27.0 1.9 all_gather.25
  29.8 62.1 %all_gather.26 = bf16[8,8192]{0,1:T(8,128)(2,1)} all-gather(bf16[8,1024]{0,1:T(8,128)(2,1)S(1)} %copy.117), channel_id=1, replica_groups=mesh['grp'=2,'ka'=8,'pb'=2] {'ka'}, dimensions={1}, use_global_device_ids=true | all-gather | bytes 147456 | tf_op jit(solution)/shard_map/all_gather | solution.py:108
  93.3 132.9 %all-gather.8.cloned.1.call-done = bf16[16,512,768]{2,1,0:T(8,128)(2,1)} async-done(((bf16[16,64,768]{2,1,0:T(8,128)(2,1)}), bf16[16,512,768]{2,1,0:T(8,128)(2,1)}) %all-gather.8.cloned.1.call-update) | async-done | bytes 12582928 | tf_op jit(solution)/shard_map/all_gather | solution.py:124
  226.2 17.7 %convert_bitcast_fusion.2 = bf16[16,768,512]{1,2,0:T(8,128)(2,1)} fusion(bf16[16,512,768]{2,1,0:T(8,128)(2,1)} %all-gather.8.cloned.1.call-done, s32[512]{0:T(512)S(1)} %bitcast.117, s32[512]{0:T(512)S(1)} %bitcast.119, s32[512]{0:T(512)S(1)} %bitcast.116, s32[512]{0:T(512)S(1)} %bitcast.120, s32[512]{0:T(512)S(1)} %bitcast.115, s32[512]{0:T(512)S(1)} %bitcast.118), kind=kOutput, calls=%fused_computation.53 | convolution fusion | flops 6452412416 | bytes 25178112 | tf_op jit(solution)/shard_map/rk,qrf->qfk/dot_general | solution.py:31
  243.8 32.1 %all-gather.4.cloned.1.call-done = bf16[64,8192]{0,1:T(8,128)(2,1)} async-done(((bf16[64,1024]{0,1:T(8,128)(2,1)}), bf16[64,8192]{0,1:T(8,128)(2,1)}) %all-gather.4.cloned.1.call-update) | async-done | bytes 1048592 | tf_op jit(solution)/shard_map/all_gather | solution.py:107
  275.9 418.6 %while.15 = (s32[]{:T(128)}, f32[8,512]{1,0:T(8,128)}, f32[16,12]{1,0:T(8,128)}, s32[16,512]{1,0:T(8,128)}, bf16[64,8192]{0,1:T(8,128)(2,1)}, /*index=5*/bf16[16...) while((s32[]{:T(128)}, f32[8,512]{1,0:T(8,128)}, ...), condition=%wide.region_3.4_spmd.clone, body=%wide.region_0.3_spmd.clone.sunk | while | flops 27432532 | bytes 23188568 | solution.py:83
  277.4 1.7 fusion.34
  283.1 2.9 gather_fusion
  288.1 2.9 gather_fusion.1
  299.6 1.9 multiply_reduce_fusion.4
  303.6 1.7 fusion.34
  309.2 2.9 gather_fusion
  314.3 2.9 gather_fusion.1
  325.8 1.9 multiply_reduce_fusion.4
  335.4 2.9 gather_fusion
  340.5 2.9 gather_fusion.1
  352.0 1.9 multiply_reduce_fusion.4
  356.0 1.7 fusion.34
  361.6 2.9 gather_fusion
  366.7 2.9 gather_fusion.1
  378.2 1.9 multiply_reduce_fusion.4
  382.2 1.7 fusion.34
  387.8 2.9 gather_fusion
  392.9 2.9 gather_fusion.1
  404.4 1.9 multiply_reduce_fusion.4
  408.4 1.7 fusion.34
  414.0 2.9 gather_fusion
  419.0 2.9 gather_fusion.1
  430.5 1.9 multiply_reduce_fusion.4
  434.5 1.7 fusion.34
  440.2 2.9 gather_fusion
  445.2 2.9 gather_fusion.1
  456.7 1.9 multiply_reduce_fusion.4
  466.3 2.9 gather_fusion
  471.4 2.9 gather_fusion.1
  482.9 1.9 multiply_reduce_fusion.4
  492.5 2.9 gather_fusion
  497.6 2.9 gather_fusion.1
  509.0 1.9 multiply_reduce_fusion.4
  518.7 2.9 gather_fusion
  523.7 2.9 gather_fusion.1
  535.2 1.9 multiply_reduce_fusion.4
  544.8 2.9 gather_fusion
  549.9 2.9 gather_fusion.1
  561.3 1.9 multiply_reduce_fusion.4
  570.9 2.9 gather_fusion
  576.0 2.9 gather_fusion.1
  587.5 1.9 multiply_reduce_fusion.4
  597.1 2.9 gather_fusion
  602.1 2.9 gather_fusion.1
  613.6 1.9 multiply_reduce_fusion.4
  623.2 2.9 gather_fusion
  628.3 2.9 gather_fusion.1
  639.7 1.9 multiply_reduce_fusion.4
  649.4 2.9 gather_fusion
  654.4 2.9 gather_fusion.1
  665.9 1.9 multiply_reduce_fusion.4
  675.5 2.9 gather_fusion
  680.6 2.9 gather_fusion.1
  692.0 1.9 multiply_reduce_fusion.4
  695.3 1.8 all_gather.27
  697.1 31.7 %psum.7 = f32[16,12]{1,0:T(8,128)S(1)} all-reduce(f32[16,12]{1,0:T(8,128)} %get-tuple-element.165), channel_id=1, replica_groups=mesh['grp'=2,'ka'=8,'pb'=2] {'ka','pb'}, use_global_device_ids=true, to_apply=%region_4.5 | all-reduce | flops 192 | bytes 1536 | tf_op jit(solution)/shard_map/psum | solution.py:139
  (872 shorter events, 288.7 us)
Async XLA Ops:
  7.2 15.0 %copy-start.10 = (bf16[64,1024]{1,0:T(8,128)(2,1)S(1)}, bf16[64,1024]{1,0:T(8,128)(2,1)}, u32[]{:S(2)}) copy-start(bf16[64,1024]{1,0:T(8,128)(2,1)} %param.14) | copy-start | bytes 393220
  7.2 16.0 %copy-start.12 = (s32[8,1024]{1,0:T(8,128)S(1)}, s32[8,1024]{1,0:T(8,128)}, u32[]{:S(2)}) copy-start(s32[8,1024]{1,0:T(8,128)} %param.16) | copy-start | bytes 98308
  7.2 18.5 %copy-start.11 = (bf16[8,1024]{1,0:T(8,128)(2,1)S(1)}, bf16[8,1024]{1,0:T(8,128)(2,1)}, u32[]{:S(2)}) copy-start(bf16[8,1024]{1,0:T(8,128)(2,1)} %param.15) | copy-start | bytes 49156
  7.2 19.8 %copy-start.14 = (bf16[8,12]{1,0:T(8,128)(2,1)S(1)}, bf16[8,12]{1,0:T(8,128)(2,1)}, u32[]{:S(2)}) copy-start(bf16[8,12]{1,0:T(8,128)(2,1)} %param.17) | copy-start | bytes 580
  7.2 14.9 %all-gather.6.cloned.1.call-start = ((), (), s32[]{:S(2)}) async-start(), calls=%async_computation.1 | async-start | bytes 2359296 | tf_op jit(solution)/shard_map/all_gather | solution.py:111
  7.9 218.2 %all-gather.8.cloned.1.call-start = ((), (), s32[]{:S(2)}) async-start(), calls=%async_computation.2 | async-start | bytes 14155776 | tf_op jit(solution)/shard_map/all_gather | solution.py:124
  22.1 253.8 %all-gather.4.cloned.1.call-start = ((), (), s32[]{:S(2)}) async-start(), calls=%async_computation | async-start | bytes 2359296 | tf_op jit(solution)/shard_map/all_gather | solution.py:107
  23.1 70.2 %copy-start.13 = (s32[512,3]{0,1:T(4,128)S(1)}, s32[512,3]{0,1:T(4,128)}, u32[]{:S(2)}) copy-start(s32[512,3]{0,1:T(4,128)} %param.12) | copy-start | bytes 18436
  275.9 10.8 %copy-start.4 = (f32[8,512]{1,0:T(8,128)}, f32[8,512]{1,0:T(8,128)S(1)}, u32[]{:S(2)}) copy-start(f32[8,512]{1,0:T(8,128)S(1)} %get-tuple-element.574) | copy-start | bytes 49156 | tf_op jit(solution)/shard_map/while
  275.9 10.8 %copy-start.6 = (f32[8,512]{1,0:T(8,128)}, f32[8,512]{1,0:T(8,128)S(1)}, u32[]{:S(2)}) copy-start(f32[8,512]{1,0:T(8,128)S(1)} %get-tuple-element.575) | copy-start | bytes 49156 | tf_op jit(solution)/shard_map/while
  294.4 5.1 copy-start.3
  297.5 4.6 copy-start.7
  302.1 10.8 %copy-start.4 = (f32[8,512]{1,0:T(8,128)}, f32[8,512]{1,0:T(8,128)S(1)}, u32[]{:S(2)}) copy-start(f32[8,512]{1,0:T(8,128)S(1)} %get-tuple-element.574) | copy-start | bytes 49156 | tf_op jit(solution)/shard_map/while
  302.1 10.8 %copy-start.6 = (f32[8,512]{1,0:T(8,128)}, f32[8,512]{1,0:T(8,128)S(1)}, u32[]{:S(2)}) copy-start(f32[8,512]{1,0:T(8,128)S(1)} %get-tuple-element.575) | copy-start | bytes 49156 | tf_op jit(solution)/shard_map/while
  320.6 5.1 copy-start.3
  323.7 4.6 copy-start.7
  328.3 10.8 %copy-start.4 = (f32[8,512]{1,0:T(8,128)}, f32[8,512]{1,0:T(8,128)S(1)}, u32[]{:S(2)}) copy-start(f32[8,512]{1,0:T(8,128)S(1)} %get-tuple-element.574) | copy-start | bytes 49156 | tf_op jit(solution)/shard_map/while
  328.3 10.8 %copy-start.6 = (f32[8,512]{1,0:T(8,128)}, f32[8,512]{1,0:T(8,128)S(1)}, u32[]{:S(2)}) copy-start(f32[8,512]{1,0:T(8,128)S(1)} %get-tuple-element.575) | copy-start | bytes 49156 | tf_op jit(solution)/shard_map/while
  346.7 5.1 copy-start.3
  349.9 4.6 copy-start.7
  354.5 10.8 %copy-start.4 = (f32[8,512]{1,0:T(8,128)}, f32[8,512]{1,0:T(8,128)S(1)}, u32[]{:S(2)}) copy-start(f32[8,512]{1,0:T(8,128)S(1)} %get-tuple-element.574) | copy-start | bytes 49156 | tf_op jit(solution)/shard_map/while
  354.5 10.8 %copy-start.6 = (f32[8,512]{1,0:T(8,128)}, f32[8,512]{1,0:T(8,128)S(1)}, u32[]{:S(2)}) copy-start(f32[8,512]{1,0:T(8,128)S(1)} %get-tuple-element.575) | copy-start | bytes 49156 | tf_op jit(solution)/shard_map/while
  372.9 5.1 copy-start.3
  376.1 4.6 copy-start.7
  380.7 10.8 %copy-start.4 = (f32[8,512]{1,0:T(8,128)}, f32[8,512]{1,0:T(8,128)S(1)}, u32[]{:S(2)}) copy-start(f32[8,512]{1,0:T(8,128)S(1)} %get-tuple-element.574) | copy-start | bytes 49156 | tf_op jit(solution)/shard_map/while
  380.7 10.8 %copy-start.6 = (f32[8,512]{1,0:T(8,128)}, f32[8,512]{1,0:T(8,128)S(1)}, u32[]{:S(2)}) copy-start(f32[8,512]{1,0:T(8,128)S(1)} %get-tuple-element.575) | copy-start | bytes 49156 | tf_op jit(solution)/shard_map/while
  399.1 5.1 copy-start.3
  402.2 4.6 copy-start.7
  406.9 10.8 %copy-start.4 = (f32[8,512]{1,0:T(8,128)}, f32[8,512]{1,0:T(8,128)S(1)}, u32[]{:S(2)}) copy-start(f32[8,512]{1,0:T(8,128)S(1)} %get-tuple-element.574) | copy-start | bytes 49156 | tf_op jit(solution)/shard_map/while
  406.9 10.8 %copy-start.6 = (f32[8,512]{1,0:T(8,128)}, f32[8,512]{1,0:T(8,128)S(1)}, u32[]{:S(2)}) copy-start(f32[8,512]{1,0:T(8,128)S(1)} %get-tuple-element.575) | copy-start | bytes 49156 | tf_op jit(solution)/shard_map/while
  425.3 5.1 copy-start.3
  428.4 4.6 copy-start.7
  433.1 10.8 %copy-start.4 = (f32[8,512]{1,0:T(8,128)}, f32[8,512]{1,0:T(8,128)S(1)}, u32[]{:S(2)}) copy-start(f32[8,512]{1,0:T(8,128)S(1)} %get-tuple-element.574) | copy-start | bytes 49156 | tf_op jit(solution)/shard_map/while
  433.1 10.8 %copy-start.6 = (f32[8,512]{1,0:T(8,128)}, f32[8,512]{1,0:T(8,128)S(1)}, u32[]{:S(2)}) copy-start(f32[8,512]{1,0:T(8,128)S(1)} %get-tuple-element.575) | copy-start | bytes 49156 | tf_op jit(solution)/shard_map/while
  451.5 5.1 copy-start.3
  454.6 4.6 copy-start.7
  459.2 10.8 %copy-start.4 = (f32[8,512]{1,0:T(8,128)}, f32[8,512]{1,0:T(8,128)S(1)}, u32[]{:S(2)}) copy-start(f32[8,512]{1,0:T(8,128)S(1)} %get-tuple-element.574) | copy-start | bytes 49156 | tf_op jit(solution)/shard_map/while
  459.2 10.8 %copy-start.6 = (f32[8,512]{1,0:T(8,128)}, f32[8,512]{1,0:T(8,128)S(1)}, u32[]{:S(2)}) copy-start(f32[8,512]{1,0:T(8,128)S(1)} %get-tuple-element.575) | copy-start | bytes 49156 | tf_op jit(solution)/shard_map/while
  477.6 5.1 copy-start.3
  480.8 4.6 copy-start.7
  485.4 10.8 %copy-start.4 = (f32[8,512]{1,0:T(8,128)}, f32[8,512]{1,0:T(8,128)S(1)}, u32[]{:S(2)}) copy-start(f32[8,512]{1,0:T(8,128)S(1)} %get-tuple-element.574) | copy-start | bytes 49156 | tf_op jit(solution)/shard_map/while
  485.4 10.8 %copy-start.6 = (f32[8,512]{1,0:T(8,128)}, f32[8,512]{1,0:T(8,128)S(1)}, u32[]{:S(2)}) copy-start(f32[8,512]{1,0:T(8,128)S(1)} %get-tuple-element.575) | copy-start | bytes 49156 | tf_op jit(solution)/shard_map/while
  503.8 5.1 copy-start.3
  511.6 10.8 %copy-start.4 = (f32[8,512]{1,0:T(8,128)}, f32[8,512]{1,0:T(8,128)S(1)}, u32[]{:S(2)}) copy-start(f32[8,512]{1,0:T(8,128)S(1)} %get-tuple-element.574) | copy-start | bytes 49156 | tf_op jit(solution)/shard_map/while
  511.6 10.8 %copy-start.6 = (f32[8,512]{1,0:T(8,128)}, f32[8,512]{1,0:T(8,128)S(1)}, u32[]{:S(2)}) copy-start(f32[8,512]{1,0:T(8,128)S(1)} %get-tuple-element.575) | copy-start | bytes 49156 | tf_op jit(solution)/shard_map/while
  530.0 5.1 copy-start.3
  537.7 10.8 %copy-start.4 = (f32[8,512]{1,0:T(8,128)}, f32[8,512]{1,0:T(8,128)S(1)}, u32[]{:S(2)}) copy-start(f32[8,512]{1,0:T(8,128)S(1)} %get-tuple-element.574) | copy-start | bytes 49156 | tf_op jit(solution)/shard_map/while
  537.7 10.8 %copy-start.6 = (f32[8,512]{1,0:T(8,128)}, f32[8,512]{1,0:T(8,128)S(1)}, u32[]{:S(2)}) copy-start(f32[8,512]{1,0:T(8,128)S(1)} %get-tuple-element.575) | copy-start | bytes 49156 | tf_op jit(solution)/shard_map/while
  556.1 5.1 copy-start.3
  563.8 10.8 %copy-start.4 = (f32[8,512]{1,0:T(8,128)}, f32[8,512]{1,0:T(8,128)S(1)}, u32[]{:S(2)}) copy-start(f32[8,512]{1,0:T(8,128)S(1)} %get-tuple-element.574) | copy-start | bytes 49156 | tf_op jit(solution)/shard_map/while
  563.8 10.8 %copy-start.6 = (f32[8,512]{1,0:T(8,128)}, f32[8,512]{1,0:T(8,128)S(1)}, u32[]{:S(2)}) copy-start(f32[8,512]{1,0:T(8,128)S(1)} %get-tuple-element.575) | copy-start | bytes 49156 | tf_op jit(solution)/shard_map/while
  582.2 5.1 copy-start.3
  590.0 10.8 %copy-start.4 = (f32[8,512]{1,0:T(8,128)}, f32[8,512]{1,0:T(8,128)S(1)}, u32[]{:S(2)}) copy-start(f32[8,512]{1,0:T(8,128)S(1)} %get-tuple-element.574) | copy-start | bytes 49156 | tf_op jit(solution)/shard_map/while
  590.0 10.8 %copy-start.6 = (f32[8,512]{1,0:T(8,128)}, f32[8,512]{1,0:T(8,128)S(1)}, u32[]{:S(2)}) copy-start(f32[8,512]{1,0:T(8,128)S(1)} %get-tuple-element.575) | copy-start | bytes 49156 | tf_op jit(solution)/shard_map/while
  608.4 5.1 copy-start.3
  616.1 10.8 %copy-start.4 = (f32[8,512]{1,0:T(8,128)}, f32[8,512]{1,0:T(8,128)S(1)}, u32[]{:S(2)}) copy-start(f32[8,512]{1,0:T(8,128)S(1)} %get-tuple-element.574) | copy-start | bytes 49156 | tf_op jit(solution)/shard_map/while
  616.1 10.8 %copy-start.6 = (f32[8,512]{1,0:T(8,128)}, f32[8,512]{1,0:T(8,128)S(1)}, u32[]{:S(2)}) copy-start(f32[8,512]{1,0:T(8,128)S(1)} %get-tuple-element.575) | copy-start | bytes 49156 | tf_op jit(solution)/shard_map/while
  634.5 5.1 copy-start.3
  642.2 10.8 %copy-start.4 = (f32[8,512]{1,0:T(8,128)}, f32[8,512]{1,0:T(8,128)S(1)}, u32[]{:S(2)}) copy-start(f32[8,512]{1,0:T(8,128)S(1)} %get-tuple-element.574) | copy-start | bytes 49156 | tf_op jit(solution)/shard_map/while
  642.3 10.8 %copy-start.6 = (f32[8,512]{1,0:T(8,128)}, f32[8,512]{1,0:T(8,128)S(1)}, u32[]{:S(2)}) copy-start(f32[8,512]{1,0:T(8,128)S(1)} %get-tuple-element.575) | copy-start | bytes 49156 | tf_op jit(solution)/shard_map/while
  660.7 5.1 copy-start.3
  668.4 10.8 %copy-start.4 = (f32[8,512]{1,0:T(8,128)}, f32[8,512]{1,0:T(8,128)S(1)}, u32[]{:S(2)}) copy-start(f32[8,512]{1,0:T(8,128)S(1)} %get-tuple-element.574) | copy-start | bytes 49156 | tf_op jit(solution)/shard_map/while
  668.4 10.8 %copy-start.6 = (f32[8,512]{1,0:T(8,128)}, f32[8,512]{1,0:T(8,128)S(1)}, u32[]{:S(2)}) copy-start(f32[8,512]{1,0:T(8,128)S(1)} %get-tuple-element.575) | copy-start | bytes 49156 | tf_op jit(solution)/shard_map/while
  686.8 5.1 copy-start.3
  (104 other events, 269.3 us)
Sparse Core Ops, SparseCore 0:
  9.6 12.4 all-gather.5
  24.3 201.7 all-gather.7
  228.3 47.6 all-gather.3
where the time goes:
time: 743 us; the launch traced here: 737 us
  local copies, waits for them, and re-layouts  266 us (36%)
  waiting for transfers between devices  180 us (24%)
  other arithmetic  155 us (21%)
  blocking collectives  99.4 us (13%)
  matrix products  17.7 us (2%)
  between operations  15.2 us (2%)
    all_gather x1, waiting for transfers between devices, on_device(): lax.all_gather(coupling_all, 'ka', axis=1, tiled=True)  133 us
    all_gather x1, blocking collectives, on_device(): lax.all_gather(quasiparticle_level_offsets, 'ka', axis=1, tiled=True)  62.1 us
    gather x32, local copies, waits for them, and re-layouts, advance(): e_far = jnp.take(en_all, kq_rows, axis=1).astype(jnp.float32)  47.8 us
    gather x16, local copies, waits for them, and re-layouts, advance(): jnp.take(eig_all, kq_rows, axis=1).astype(jnp.float32)  46.6 us
    slice x112, local copies, waits for them, and re-layouts, advance(): u_far[index_a][None, :, None, :] * inner[:, index_a][:, None, :, :]  36.2 us
    all_gather x1, waiting for transfers between devices, on_device(): lax.all_gather(unitary_band_mixer, 'ka', axis=1, tiled=True)  32.1 us
    psum x1, blocking collectives, on_device(): widths = lax.psum(widths, ('ka', 'pb'))  31.7 us
    reduce_sum x16, other arithmetic, advance(): self_term = jnp.sum(squared * kpoint_weight, axis=(0, 1))  30 us
  transfers between devices with their start and end apart: 3, of which 3 were waited for; matrix products, arithmetic and copies ran while one was open for 3% of the time, Pallas kernels for 0%

commit v1 on v0

v1 whole, which is shorter than its diff:
```python
import functools
import math

import jax
import jax.numpy as jnp
from jax import lax
from jax.experimental import pallas as pl
from jax.experimental.pallas import tpu as pltpu
from jax.sharding import PartitionSpec as P

NB = 8
NM = 12
ETA = 0.05
ROWS = 80
MESH = pl.DeviceIdType.MESH
SIN = (6.28318516, -41.3416549, 81.6009982, -76.5496568, 39.5358137)


def exchange(pack_ref, table_ref, all_ref, part_ref, send_pack, recv_pack, send_part, recv_part, own_sems):
    count = all_ref.shape[0]
    per_q = count // table_ref.shape[0]
    me = lax.axis_index("ka")
    barrier = pltpu.get_barrier_semaphore()

    def greet(step, carry):
        pl.semaphore_signal(barrier, inc=1, device_id={"ka": lax.rem(me + step, count)}, device_id_type=MESH)
        return carry

    lax.fori_loop(1, count, greet, 0)
    pl.semaphore_wait(barrier, count - 1)

    def copies(step, sender):
        peer = lax.rem(me + step, count)
        block = pltpu.make_async_remote_copy(
            src_ref=pack_ref,
            dst_ref=all_ref.at[sender],
            send_sem=send_pack.at[step],
            recv_sem=recv_pack.at[sender],
            device_id={"ka": peer},
            device_id_type=MESH,
        )
        cells = pltpu.make_async_remote_copy(
            src_ref=table_ref.at[peer // per_q],
            dst_ref=part_ref.at[sender],
            send_sem=send_part.at[step],
            recv_sem=recv_part.at[sender],
            device_id={"ka": peer},
            device_id_type=MESH,
        )
        return block, cells

    def start(step, carry):
        block, cells = copies(step, me)
        block.start()
        cells.start()
        return carry

    lax.fori_loop(1, count, start, 0)
    own = (
        pltpu.make_async_copy(pack_ref, all_ref.at[me], own_sems.at[0]),
        pltpu.make_async_copy(table_ref.at[me // per_q], part_ref.at[me], own_sems.at[1]),
    )
    for copy in own:
        copy.start()
    for copy in own:
        copy.wait()

    def finish(step, carry):
        block, cells = copies(step, me)
        block.wait_send()
        cells.wait_send()
        block, cells = copies(step, lax.rem(me + step, count))
        block.wait_recv()
        cells.wait_recv()
        return carry

    lax.fori_loop(1, count, finish, 0)


def couple(
    where_ref,
    mode_ref,
    all_ref,
    part_ref,
    cell_ref,
    sigma_ref,
    width_ref,
    interp,
    near,
    far,
    level,
    acc,
):
    block = where_ref[1] + pl.program_id(0)
    chunks = all_ref.shape[0] * 8
    inv_t = mode_ref[3, 0]

    @pl.when(pl.program_id(0) == 0)
    def _():
        acc[...] = jnp.zeros_like(acc)

    product = jnp.dot(cell_ref[...], all_ref[block, 64:80, :], preferred_element_type=jnp.float32)
    turn = product * 0.01
    turn = jnp.abs(turn - jnp.floor(turn + 0.5))
    angle = 0.25 - turn
    square = angle * angle
    value = SIN[4]
    for coefficient in (SIN[3], SIN[2], SIN[1], SIN[0]):
        value = value * square + coefficient
    phase = (value * angle).astype(jnp.bfloat16)
    folded = lax.dot_general(part_ref[...], phase, (((0,), (0,)), ((), ())), preferred_element_type=jnp.float32)
    for c in range(8):
        interp[pl.ds(c, 64 * NM, stride=8), :] = folded[:, c * 128 : (c + 1) * 128]

    for c in range(8):
        near[pl.ds(c, ROWS, stride=8), :] = all_ref[block, :, c * 128 : (c + 1) * 128].astype(jnp.float32)
    offset = lax.rem(block * 1024 + where_ref[0], chunks * 128)
    first, inside = offset // 128, lax.rem(offset, 128)
    lanes = lax.broadcasted_iota(jnp.int32, (ROWS, 128), 1)

    def turned(c):
        index = lax.rem(first + c, chunks)
        lane = pl.multiple_of(lax.rem(index, 8) * 128, 128)
        raw = all_ref[index // 8, :, pl.ds(lane, 128)].astype(jnp.float32)
        return pltpu.roll(raw, lax.rem(128 - inside, 128), 1)

    here = turned(0)
    for c in range(8):
        after = turned(c + 1)
        far[pl.ds(c, ROWS, stride=8), :] = jnp.where(lanes < 128 - inside, here, after)
        here = after

    def row(ref, index):
        return ref[pl.ds(pl.multiple_of(index * 8, 8), 8), :]

    def fermi(energy):
        return 1.0 / (1.0 + jnp.exp(energy * inv_t))

    for m in range(NB):
        level[pl.ds(m * 8, 8), :] = fermi(row(far, 64 + m))
    tally = row(near, 75)

    def over_n(n, carry):
        e_n = row(near, 64 + n)
        f_n = fermi(e_n)
        mask = jnp.where(n.astype(jnp.float32) < tally, 1.0, 0.0)
        for m in range(NB):
            gap = e_n - row(far, 64 + m)
            level[pl.ds(64 + m * 8, 8), :] = gap * gap + ETA * ETA
            level[pl.ds(128 + m * 8, 8), :] = gap + gap
            level[pl.ds(192 + m * 8, 8), :] = mask * (f_n - row(level, m))
            level[pl.ds(256 + m * 8, 8), :] = (1.0 - 2.0 * row(level, m)) * (gap + gap)
        u_n = [row(near, b * NB + n) for b in range(NB)]

        def over_v(v, total):
            w = mode_ref[0, v]
            w2 = mode_ref[1, v]
            twice = mode_ref[2, v]
            inner = []
            for a in range(NB):
                term = row(interp, v * 64 + a * 8) * u_n[0]
                for b in range(1, NB):
                    term = term + row(interp, v * 64 + a * 8 + b) * u_n[b]
                inner.append(term)
            width = jnp.zeros((8, 128), jnp.float32)
            for m in range(NB):
                rotated = row(far, m) * inner[0]
                for a in range(1, NB):
                    rotated = rotated + row(far, a * NB + m) * inner[a]
                even = row(level, 8 + m) + w2
                odd = row(level, 16 + m) * w
                low = even - odd
                high = even + odd
                scaled = rotated * rotated * pl.reciprocal(low * high)
                total = total + scaled * (twice * even + w * row(level, 32 + m))
                width = width + row(level, 24 + m) * (low * scaled)
            spot = pl.ds(pl.multiple_of(v * 8, 8), 8)
            acc[spot, :] = acc[spot, :] + width
            return total

        total = lax.fori_loop(0, NM, over_v, jnp.zeros((8, 128), jnp.float32))
        sigma_ref[0, pl.ds(pl.multiple_of(n * 8, 8), 8), :] = mask * total
        return carry

    lax.fori_loop(0, NB, over_n, 0)

    @pl.when(pl.program_id(0) == pl.num_programs(0) - 1)
    def _():
        lane = lax.broadcasted_iota(jnp.int32, (8, 128), 1)
        out = jnp.zeros((8, 128), jnp.float32)
        for v in range(NM):
            out = out + jnp.where(lane == v, jnp.sum(acc[v * 8 : v * 8 + 8, :]), 0.0)
        width_ref[...] = out


def collect(q_local, sigma_ref, width_ref, total_ref, widths_ref, got, got_w, send_s, recv_s, send_w, recv_w, own_sems):
    count = got_w.shape[0]
    cores = got.shape[0] // q_local
    per_q = count // q_local
    me, core = lax.axis_index("ka"), lax.axis_index("pb")
    everyone = count * cores
    mine = me * cores + core
    barrier = pltpu.get_barrier_semaphore()

    def greet(step, carry):
        other = lax.rem(mine + step, everyone)
        pl.semaphore_signal(
            barrier, inc=1, device_id={"ka": other // cores, "pb": lax.rem(other, cores)}, device_id_type=MESH
        )
        return carry

    lax.fori_loop(1, everyone, greet, 0)
    pl.semaphore_wait(barrier, everyone - 1)

    q_mine, range_mine = me // per_q, lax.rem(me, per_q)
    slot_mine = core * q_local + q_mine

    def sigma_copy(index, slot):
        b, to_core = index // cores, lax.rem(index, cores)
        return pltpu.make_async_remote_copy(
            src_ref=sigma_ref.at[b],
            dst_ref=got.at[slot],
            send_sem=send_s.at[index],
            recv_sem=recv_s.at[slot],
            device_id={"ka": range_mine * q_local + b, "pb": to_core},
            device_id_type=MESH,
        )

    def width_copy(step, sender):
        return pltpu.make_async_remote_copy(
            src_ref=width_ref,
            dst_ref=got_w.at[sender],
            send_sem=send_w.at[step],
            recv_sem=recv_w.at[sender],
            device_id={"ka": lax.rem(me + step, count)},
            device_id_type=MESH,
        )

    def start_s(index, carry):
        target = (range_mine * q_local + index // cores) * cores + lax.rem(index, cores)

        @pl.when(target != mine)
        def _():
            sigma_copy(index, slot_mine).start()

        @pl.when(target == mine)
        def _():
            copy = pltpu.make_async_copy(sigma_ref.at[index // cores], got.at[slot_mine], own_sems.at[0])
            copy.start()
            copy.wait()

        return carry

    lax.fori_loop(0, q_local * cores, start_s, 0)

    def start_w(step, carry):
        width_copy(step, me).start()
        return carry

    lax.fori_loop(1, count, start_w, 0)
    copy = pltpu.make_async_copy(width_ref, got_w.at[me], own_sems.at[1])
    copy.start()
    copy.wait()

    def finish_s(index, carry):
        target = (range_mine * q_local + index // cores) * cores + lax.rem(index, cores)

        @pl.when(target != mine)
        def _():
            sigma_copy(index, slot_mine).wait_send()

        from_core, from_q = index // q_local, lax.rem(index, q_local)
        source = (from_q * per_q + me // q_local) * cores + from_core

        @pl.when(source != mine)
        def _():
            sigma_copy(index, index).wait_recv()

        return carry

    lax.fori_loop(0, q_local * cores, finish_s, 0)

    def finish_w(step, carry):
        width_copy(step, me).wait_send()
        width_copy(step, lax.rem(me + step, count)).wait_recv()
        return carry

    lax.fori_loop(1, count, finish_w, 0)
    total = got[0]
    for slot in range(1, q_local * cores):
        total = total + got[slot]
    total_ref[...] = total
    for q in range(q_local):
        width = got_w[q * per_q]
        for part in range(1, per_q):
            width = width + got_w[q * per_q + part]
        widths_ref[q, :, :] = width


def on_device(
    momentum_mesh_positions,
    bravais_translation_list,
    localized_matrix_element_table,
    unitary_band_mixer,
    quasiparticle_level_offsets,
    displaced_momentum_slot,
    vibration_mode_pulsations,
    occupied_band_tally,
    heat_bath_scale,
):
    kcount = momentum_mesh_positions.shape[1]
    q_local, cells, feat = localized_matrix_element_table.shape
    count, cores = lax.axis_size("ka"), lax.axis_size("pb")
    k_total = kcount * count
    per_q = count // q_local
    me = lax.axis_index("ka")
    tau = heat_bath_scale[0]
    pack = jnp.concatenate(
        [
            unitary_band_mixer,
            quasiparticle_level_offsets,
            momentum_mesh_positions.astype(jnp.bfloat16),
            jnp.broadcast_to(occupied_band_tally.astype(jnp.bfloat16)[:, None], (1, kcount)),
            jnp.zeros((4, kcount), jnp.bfloat16),
        ],
        axis=0,
    )
    q_mine = me // per_q
    slot = lax.dynamic_slice(displaced_momentum_slot, (q_mine, 0), (1, 1))[0, 0]
    shift = jnp.mod(slot - me * kcount, k_total)
    where = jnp.stack([shift, lax.rem(me, per_q) * q_local]).astype(jnp.int32)
    freq_own = vibration_mode_pulsations.astype(jnp.float32)
    freq = lax.dynamic_slice_in_dim(freq_own, q_mine, 1, 0)[0]
    twice = 2.0 / (jnp.exp(freq / tau) - 1.0) + 1.0
    modes = jnp.stack([freq, freq * freq, twice, jnp.broadcast_to(1.0 / tau, (NM,))])
    cell_rows = jnp.pad(bravais_translation_list.astype(jnp.bfloat16), ((0, 0), (8, 5)))

    anywhere = pl.BlockSpec(memory_space=pl.ANY)
    in_vmem = pl.BlockSpec(memory_space=pltpu.VMEM)
    in_smem = pl.BlockSpec(memory_space=pltpu.SMEM)
    packs, part = pl.pallas_call(
        exchange,
        out_shape=(
            jax.ShapeDtypeStruct((count, ROWS, kcount), jnp.bfloat16),
            jax.ShapeDtypeStruct((count, cells, feat), jnp.bfloat16),
        ),
        in_specs=[anywhere] * 2,
        out_specs=(anywhere, anywhere),
        scratch_shapes=[pltpu.SemaphoreType.DMA((count,))] * 4 + [pltpu.SemaphoreType.DMA((2,))],
        compiler_params=pltpu.CompilerParams(collective_id=0, has_side_effects=True),
    )(pack, localized_matrix_element_table)

    sigma, width = pl.pallas_call(
        couple,
        grid=(q_local,),
        out_shape=(
            jax.ShapeDtypeStruct((q_local, NB * 8, 128), jnp.float32),
            jax.ShapeDtypeStruct((8, 128), jnp.float32),
        ),
        in_specs=[in_smem, in_smem, in_vmem, in_vmem, in_vmem],
        out_specs=(
            pl.BlockSpec((1, NB * 8, 128), lambda i: (i, 0, 0)),
            pl.BlockSpec((8, 128), lambda i: (0, 0)),
        ),
        scratch_shapes=[
            pltpu.VMEM((64 * NM * 8, 128), jnp.float32),
            pltpu.VMEM((ROWS * 8, 128), jnp.float32),
            pltpu.VMEM((ROWS * 8, 128), jnp.float32),
            pltpu.VMEM((5 * 64, 128), jnp.float32),
            pltpu.VMEM((NM * 8, 128), jnp.float32),
        ],
        compiler_params=pltpu.CompilerParams(vmem_limit_bytes=48 * 1024 * 1024),
    )(where, modes, packs, part.reshape(count * cells, feat), cell_rows)

    total, widths = pl.pallas_call(
        functools.partial(collect, q_local),
        out_shape=(
            jax.ShapeDtypeStruct((NB * 8, 128), jnp.float32),
            jax.ShapeDtypeStruct((q_local, 8, 128), jnp.float32),
        ),
        in_specs=[in_vmem] * 2,
        out_specs=(in_vmem, in_vmem),
        scratch_shapes=[
            pltpu.VMEM((cores * q_local, NB * 8, 128), jnp.float32),
            pltpu.VMEM((count, 8, 128), jnp.float32),
            pltpu.SemaphoreType.DMA((cores * q_local,)),
            pltpu.SemaphoreType.DMA((cores * q_local,)),
            pltpu.SemaphoreType.DMA((count,)),
            pltpu.SemaphoreType.DMA((count,)),
            pltpu.SemaphoreType.DMA((2,)),
        ],
        compiler_params=pltpu.CompilerParams(collective_id=1, has_side_effects=True),
    )(sigma, width)
    scale = ETA / math.pi
    self_energy = total.reshape(NB, kcount) * (scale / (q_local * cores * NM))
    linewidth = widths[:, 0, :NM] * freq_own * (2.0 * math.pi * scale / k_total)
    return (self_energy, linewidth)


def solution(mesh):
    return jax.shard_map(
        on_device,
        mesh=mesh,
        in_specs=(
            P(None, "ka"),
            P(),
            P(("grp", "pb"), "ka", None),
            P(None, ("grp", "ka")),
            P(None, ("grp", "ka")),
            P(("grp", "pb"), "ka"),
            P(("grp", "pb"), None),
            P(("grp", "ka")),
            P("grp"),
        ),
        out_specs=(P(None, ("grp", "ka")), P(("grp", "pb"), None)),
        check_vma=False,
    )
```

time: 743 us -> 152 us (0.20)
  local copies, waits for them, and re-layouts: 266 us -> 9.52 us
  waiting for transfers between devices: 180 us -> 0 us
  other arithmetic: 155 us -> 3.65 us
  Pallas kernels: 0 us -> 135 us
  blocking collectives: 99.4 us -> 0 us
  matrix products: 17.7 us -> 0 us
  between operations: 15.2 us -> 2.73 us
    all_gather x3 -> x0, waiting for transfers between devices: 179 us -> none  [the longest x1 133 us: on_device(): lax.all_gather(coupling_all, 'ka', axis=1, tiled=True)]
    pallas_call x0 -> x3, Pallas kernels: none -> 135 us  [the longest x1 64 us: on_device(): pl.pallas_call(couple, grid=(q_local,), out_shape=(jax.ShapeDtypeStruct((...]
    gather x48 -> x0, local copies, waits for them, and re-layouts: 94.3 us -> none  [the longest x32 47.8 us: advance(): e_far = jnp.take(en_all, kq_rows, axis=1).astype(jnp.float32)]
    slice x162 -> x1, local copies, waits for them, and re-layouts: 85.1 us -> 0.76 us  [on_device(): linewidth = widths[:, 0, :NM] * freq_own * (2.0 * math.pi * scale / k_total)]
    all_gather x4 -> x0, blocking collectives: 67.7 us -> none  [the longest x1 62.1 us: on_device(): lax.all_gather(quasiparticle_level_offsets, 'ka', axis=1, tiled=True)]
    reduce_sum x32 -> x0, other arithmetic: 51.4 us -> none  [the longest x16 30 us: advance(): self_term = jnp.sum(squared * kpoint_weight, axis=(0, 1))]
    psum x1 -> x0, blocking collectives: 31.7 us -> none  [on_device(): widths = lax.psum(widths, ('ka', 'pb'))]
    mul x32 -> x3, other arithmetic: 32.6 us -> 1.37 us  [the longest x1 0.76 us: on_device(): self_energy = total.reshape(NB, kcount) * (scale / (q_local * cores * NM))]
  transfers between devices with their start and end apart: 3 -> 0, of which waited for: 3 -> 0; matrix products, arithmetic and copies ran while one was open for 3% -> 0% of each run, Pallas kernels for 0% -> 0%
where the time goes in v1:
time: 152 us; the launch traced here: 151 us
  Pallas kernels  135 us (89%)
  local copies, waits for them, and re-layouts  9.52 us (6%)
  other arithmetic  3.65 us (2%)
  between operations  2.73 us (2%)
    pallas_call x1, Pallas kernels, on_device(): pl.pallas_call(couple, grid=(q_local,), out_shape=(jax.ShapeDtypeStruct((...  64 us
    pallas_call x1, Pallas kernels, on_device(): pl.pallas_call(exchange, out_shape=(jax.ShapeDtypeStruct((count, ROWS, kc...  40.4 us
    pallas_call x1, Pallas kernels, on_device(): pl.pallas_call(functools.partial(collect, q_local), out_shape=(jax.ShapeD...  31 us
    unnamed x12, local copies, waits for them, and re-layouts  3.74 us
    concatenate x1, local copies, waits for them, and re-layouts, on_device(): jnp.concatenate([unitary_band_mixer, quasiparticle_level_offsets, momentu...  3.52 us

profile of v1, /device:TPU:0, one launch (start us, length us, event | category | flops | bytes accessed | tf_op | source)
XLA Modules:
  0.0 151.3 jit_solution(7584497863361412262)
XLA Ops:
  0.6 0.0 copy-start
  2.0 0.1 pad.8.clone
  2.1 0.0 copy-done
  2.1 0.5 constant_dynamic-slice_fusion.1
  3.3 0.1 pad_add_fusion.where_ref
  3.3 0.7 convert_element_type.17
  4.0 0.7 convert_element_type.14
  4.7 0.1 maximum_maximum_fusion.mode_ref
  4.8 0.7 convert_element_type.15
  5.6 0.2 copy.12
  5.7 0.1 pad.4.cell_ref
  5.9 3.5 %concatenate.3.pack_ref = bf16[80,1024]{1,0:T(8,128)(2,1)} concatenate(bf16[64,1024]{1,0:T(8,128)(2,1)} %param.12, bf16[8,1024]{1,0:T(8,128)(2,1)} %param.13, bf16[3,1024]{1,0:T(4,128)(2,1)S(1)} %convert_element_type.15, bf16[1,1024]{1,0:T(2,128)(2,1)S(1)} %broadcast_in_dim.12, bf16[4,1024]{1,0:T(4,128)(2,1)S(1)} %broadcast_in_dim.13), dimensions={0} | concatenate | bytes 327680 | tf_op jit(solution)/shard_map/concatenate | solution.py:318
  9.4 40.4 %shard_map.104 = (bf16[8,80,1024]{2,1,0:T(8,128)(2,1)}, bf16[8,64,768]{2,1,0:T(8,128)(2,1)}) custom-call(bf16[80,1024]{1,0:T(8,128)(2,1)} %concatenate.3.pack_ref, bf16[8,64,768]{2,1,0:T(8,128)(2,1)} %table_ref.1), custom_call_target="tpu_custom_call" | custom-call | tf_op jit(solution)/shard_map/pallas_call | solution.py:341
  49.7 0.0 copy-start.1
  49.8 1.3 copy-done.1
  51.1 0.0 copy-start.2
  51.1 1.1 copy-done.2
  52.2 0.0 copy-start.5
  52.2 64.0 %shard_map.105 = (f32[8,64,128]{2,1,0:T(8,128)S(1)}, f32[8,128]{1,0:T(8,128)S(1)}) custom-call(s32[2]{0:T(128)S(1)} %pad_add_fusion.where_ref, f32[4,12]{1,0:T(4,128)S(1)} %maximum_maximum_fusion.mode_ref, bf16[8,80,1024]{2,1,0:T(8,128)(2,1)S(1)} %copy-done.1, bf16[512,768]{1,0:T(8,128)(2,1)S(1)} %bitcast.9, bf16[512,16]{1,0:T(8,128)(2,1)S(1)} %pad.4.cell_ref), custom_call_target="tpu_custom_call" | custom-call | tf_op jit(solution)/shard_map/pallas_call | solution.py:353
  116.2 0.0 copy-start.3
  116.2 0.7 copy-done.3
  116.9 0.0 copy-start.4
  116.9 0.6 copy-done.4
  117.5 31.0 %shard_map.106 = (f32[64,128]{1,0:T(8,128)}, f32[8,8,128]{2,1,0:T(8,128)}) custom-call(f32[8,64,128]{2,1,0:T(8,128)} %copy-done.3, f32[8,128]{1,0:T(8,128)} %copy-done.4), custom_call_target="tpu_custom_call" | custom-call | tf_op jit(solution)/shard_map/pallas_call | solution.py:375
  148.6 0.8 broadcast_multiply_fusion
  149.3 0.6 mul.30
  150.0 0.8 slice.3
  150.7 0.0 copy-done.5
  150.7 0.6 multiply_multiply_fusion
  (4 shorter events, 0.0 us)
Async XLA Ops:
  0.6 1.4 copy-start
  49.7 1.3 copy-start.1
  51.1 1.1 copy-start.2
  52.2 98.5 %copy-start.5 = (bf16[8,12]{1,0:T(8,128)(2,1)S(1)}, bf16[8,12]{1,0:T(8,128)(2,1)}, u32[]{:S(2)}) copy-start(bf16[8,12]{1,0:T(8,128)(2,1)} %param.15) | copy-start | bytes 580
  116.2 0.7 copy-start.3
  116.9 0.6 copy-start.4

commit v2 on v1

--- a/solution.py
+++ b/solution.py
@@ -85,10 +85,14 @@
     cell_ref,
     sigma_ref,
     width_ref,
+    wide,
     interp,
     near,
     far,
+    u_near,
+    u_far,
     level,
+    sums,
     acc,
 ):
     block = where_ref[1] + pl.program_id(0)
@@ -109,11 +113,23 @@
         value = value * square + coefficient
     phase = (value * angle).astype(jnp.bfloat16)
     folded = lax.dot_general(part_ref[...], phase, (((0,), (0,)), ((), ())), preferred_element_type=jnp.float32)
+    for pair in range(NM // 2):
+        for half in range(2):
+            mode = 2 * pair + half
+            for c in range(8):
+                wide[pl.ds(pair * 1024 + half * 8 + c, 64, stride=16), :] = folded[
+                    mode * 64 : mode * 64 + 64, c * 128 : (c + 1) * 128
+                ]
+    interp[...] = wide[...].astype(jnp.bfloat16)
+
+    def spread(narrow_ref, c, rows):
+        narrow_ref[pl.ds(c, 16, stride=8), :] = rows[64:ROWS]
+        wide[pl.ds(c, 64, stride=16), :] = rows[0:64]
+        wide[pl.ds(8 + c, 64, stride=16), :] = rows[0:64]
+
     for c in range(8):
-        interp[pl.ds(c, 64 * NM, stride=8), :] = folded[:, c * 128 : (c + 1) * 128]
-
-    for c in range(8):
-        near[pl.ds(c, ROWS, stride=8), :] = all_ref[block, :, c * 128 : (c + 1) * 128].astype(jnp.float32)
+        spread(near, c, all_ref[block, :, c * 128 : (c + 1) * 128].astype(jnp.float32))
+    u_near[...] = wide[0:1024, :].astype(jnp.bfloat16)
     offset = lax.rem(block * 1024 + where_ref[0], chunks * 128)
     first, inside = offset // 128, lax.rem(offset, 128)
     lanes = lax.broadcasted_iota(jnp.int32, (ROWS, 128), 1)
@@ -127,62 +143,70 @@
     here = turned(0)
     for c in range(8):
         after = turned(c + 1)
-        far[pl.ds(c, ROWS, stride=8), :] = jnp.where(lanes < 128 - inside, here, after)
+        spread(far, c, jnp.where(lanes < 128 - inside, here, after))
         here = after
+    u_far[...] = wide[0:1024, :].astype(jnp.bfloat16)
 
     def row(ref, index):
         return ref[pl.ds(pl.multiple_of(index * 8, 8), 8), :]
 
+    def pair_row(ref, index):
+        return ref[pl.ds(pl.multiple_of(index * 16, 16), 16), :]
+
     def fermi(energy):
         return 1.0 / (1.0 + jnp.exp(energy * inv_t))
 
     for m in range(NB):
-        level[pl.ds(m * 8, 8), :] = fermi(row(far, 64 + m))
-    tally = row(near, 75)
+        level[pl.ds(m * 8, 8), :] = fermi(row(far, m))
+    tally = row(near, 11)
 
     def over_n(n, carry):
-        e_n = row(near, 64 + n)
+        e_n = row(near, n)
         f_n = fermi(e_n)
         mask = jnp.where(n.astype(jnp.float32) < tally, 1.0, 0.0)
         for m in range(NB):
-            gap = e_n - row(far, 64 + m)
+            gap = e_n - row(far, m)
             level[pl.ds(64 + m * 8, 8), :] = gap * gap + ETA * ETA
             level[pl.ds(128 + m * 8, 8), :] = gap + gap
             level[pl.ds(192 + m * 8, 8), :] = mask * (f_n - row(level, m))
             level[pl.ds(256 + m * 8, 8), :] = (1.0 - 2.0 * row(level, m)) * (gap + gap)
-        u_n = [row(near, b * NB + n) for b in range(NB)]
-
-        def over_v(v, total):
-            w = mode_ref[0, v]
-            w2 = mode_ref[1, v]
-            twice = mode_ref[2, v]
+        u_n = [pair_row(u_near, b * NB + n) for b in range(NB)]
+
+        def over_pairs(pair, total):
             inner = []
             for a in range(NB):
-                term = row(interp, v * 64 + a * 8) * u_n[0]
+                term = pair_row(interp, pair * 64 + a * 8) * u_n[0]
                 for b in range(1, NB):
-                    term = term + row(interp, v * 64 + a * 8 + b) * u_n[b]
+                    term = term + pair_row(interp, pair * 64 + a * 8 + b) * u_n[b]
                 inner.append(term)
-            width = jnp.zeros((8, 128), jnp.float32)
+            widths = [jnp.zeros((8, 128), jnp.float32) for _ in range(2)]
             for m in range(NB):
-                rotated = row(far, m) * inner[0]
+                rotated = pair_row(u_far, m) * inner[0]
                 for a in range(1, NB):
-                    rotated = rotated + row(far, a * NB + m) * inner[a]
-                even = row(level, 8 + m) + w2
-                odd = row(level, 16 + m) * w
-                low = even - odd
-                high = even + odd
-                scaled = rotated * rotated * pl.reciprocal(low * high)
-                total = total + scaled * (twice * even + w * row(level, 32 + m))
-                width = width + row(level, 24 + m) * (low * scaled)
-            spot = pl.ds(pl.multiple_of(v * 8, 8), 8)
-            acc[spot, :] = acc[spot, :] + width
+                    rotated = rotated + pair_row(u_far, a * NB + m) * inner[a]
+                rotated = rotated.astype(jnp.float32)
+                for half in range(2):
+                    v = 2 * pair + half
+                    w = mode_ref[0, v]
+                    own = rotated[half * 8 : half * 8 + 8]
+                    even = row(level, 8 + m) + mode_ref[1, v]
+                    odd = row(level, 16 + m) * w
+                    low = even - odd
+                    high = even + odd
+                    scaled = own * own * pl.reciprocal(low * high, approx=True)
+                    total = total + scaled * (mode_ref[2, v] * even + w * row(level, 32 + m))
+                    widths[half] = widths[half] + row(level, 24 + m) * (low * scaled)
+            for half in range(2):
+                spot = pl.ds(pl.multiple_of(pair * 16, 16) + half * 8, 8)
+                acc[spot, :] = acc[spot, :] + widths[half]
             return total
 
-        total = lax.fori_loop(0, NM, over_v, jnp.zeros((8, 128), jnp.float32))
-        sigma_ref[0, pl.ds(pl.multiple_of(n * 8, 8), 8), :] = mask * total
+        total = lax.fori_loop(0, NM // 2, over_pairs, jnp.zeros((8, 128), jnp.float32))
+        sums[pl.ds(pl.multiple_of(n * 8, 8), 8), :] = mask * total
         return carry
 
     lax.fori_loop(0, NB, over_n, 0)
+    sigma_ref[0] = sums[...].astype(jnp.bfloat16)
 
     @pl.when(pl.program_id(0) == pl.num_programs(0) - 1)
     def _():
@@ -286,9 +310,9 @@
         return carry
 
     lax.fori_loop(1, count, finish_w, 0)
-    total = got[0]
+    total = got[0].astype(jnp.float32)
     for slot in range(1, q_local * cores):
-        total = total + got[slot]
+        total = total + got[slot].astype(jnp.float32)
     total_ref[...] = total
     for q in range(q_local):
         width = got_w[q * per_q]
@@ -354,7 +378,7 @@
         couple,
         grid=(q_local,),
         out_shape=(
-            jax.ShapeDtypeStruct((q_local, NB * 8, 128), jnp.float32),
+            jax.ShapeDtypeStruct((q_local, NB * 8, 128), jnp.bfloat16),
             jax.ShapeDtypeStruct((8, 128), jnp.float32),
         ),
         in_specs=[in_smem, in_smem, in_vmem, in_vmem, in_vmem],
@@ -364,9 +388,13 @@
         ),
         scratch_shapes=[
             pltpu.VMEM((64 * NM * 8, 128), jnp.float32),
-            pltpu.VMEM((ROWS * 8, 128), jnp.float32),
-            pltpu.VMEM((ROWS * 8, 128), jnp.float32),
+            pltpu.VMEM((64 * NM * 8, 128), jnp.bfloat16),
+            pltpu.VMEM((16 * 8, 128), jnp.float32),
+            pltpu.VMEM((16 * 8, 128), jnp.float32),
+            pltpu.VMEM((64 * 16, 128), jnp.bfloat16),
+            pltpu.VMEM((64 * 16, 128), jnp.bfloat16),
             pltpu.VMEM((5 * 64, 128), jnp.float32),
+            pltpu.VMEM((NB * 8, 128), jnp.float32),
             pltpu.VMEM((NM * 8, 128), jnp.float32),
         ],
         compiler_params=pltpu.CompilerParams(vmem_limit_bytes=48 * 1024 * 1024),
@@ -381,7 +409,7 @@
         in_specs=[in_vmem] * 2,
         out_specs=(in_vmem, in_vmem),
         scratch_shapes=[
-            pltpu.VMEM((cores * q_local, NB * 8, 128), jnp.float32),
+            pltpu.VMEM((cores * q_local, NB * 8, 128), jnp.bfloat16),
             pltpu.VMEM((count, 8, 128), jnp.float32),
             pltpu.SemaphoreType.DMA((cores * q_local,)),
             pltpu.SemaphoreType.DMA((cores * q_local,)),

time: 152 us -> 159 us (1.046)
  Pallas kernels: 135 us -> 142 us
    pallas_call x1, Pallas kernels: 64 us -> 76.7 us  [on_device(): pl.pallas_call(couple, grid=(q_local,), out_shape=(jax.ShapeDtypeStruct((...]
    pallas_call x1, Pallas kernels: 31 us -> 25.3 us  [on_device(): pl.pallas_call(functools.partial(collect, q_local), out_shape=(jax.ShapeD...]
    unnamed x12 -> x14, local copies, waits for them, and re-layouts: 3.74 us -> 4.42 us
where the time goes in v2:
time: 159 us; the launch traced here: 158 us
  Pallas kernels  142 us (89%)
  local copies, waits for them, and re-layouts  10.2 us (6%)
  other arithmetic  2.94 us (2%)
  between operations  2.78 us (2%)
    pallas_call x1, Pallas kernels, on_device(): pl.pallas_call(couple, grid=(q_local,), out_shape=(jax.ShapeDtypeStruct((...  76.7 us
    pallas_call x1, Pallas kernels, on_device(): pl.pallas_call(exchange, out_shape=(jax.ShapeDtypeStruct((count, ROWS, kc...  40.4 us
    pallas_call x1, Pallas kernels, on_device(): pl.pallas_call(functools.partial(collect, q_local), out_shape=(jax.ShapeD...  25.3 us
    unnamed x14, local copies, waits for them, and re-layouts  4.42 us
    concatenate x1, local copies, waits for them, and re-layouts, on_device(): jnp.concatenate([unitary_band_mixer, quasiparticle_level_offsets, momentu...  3.52 us

profile of v2, /device:TPU:0, one launch (start us, length us, event | category | flops | bytes accessed | tf_op | source)
XLA Modules:
  0.0 158.3 jit_solution(15040853141894852680)
XLA Ops:
  0.6 0.0 copy-start
  0.6 0.0 copy-start.6
  0.7 0.7 copy-done
  1.4 0.5 constant_dynamic-slice_fusion.1
  2.6 0.1 pad_add_fusion.where_ref
  2.7 0.7 convert_element_type.14
  4.1 0.1 pad.8.clone
  4.1 0.1 maximum_maximum_fusion.mode_ref
  4.2 0.7 convert_element_type.15
  5.6 3.5 %concatenate.3.pack_ref = bf16[80,1024]{1,0:T(8,128)(2,1)} concatenate(bf16[64,1024]{1,0:T(8,128)(2,1)} %param.12, bf16[8,1024]{1,0:T(8,128)(2,1)} %param.13, bf16[3,1024]{1,0:T(4,128)(2,1)S(1)} %convert_element_type.15, bf16[1,1024]{1,0:T(2,128)(2,1)S(1)} %broadcast_in_dim.12, bf16[4,1024]{1,0:T(4,128)(2,1)S(1)} %broadcast_in_dim.13), dimensions={0} | concatenate | bytes 327680 | tf_op jit(solution)/shard_map/concatenate | solution.py:342
  9.1 40.4 %shard_map.104 = (bf16[8,80,1024]{2,1,0:T(8,128)(2,1)}, bf16[8,64,768]{2,1,0:T(8,128)(2,1)}) custom-call(bf16[80,1024]{1,0:T(8,128)(2,1)} %concatenate.3.pack_ref, bf16[8,64,768]{2,1,0:T(8,128)(2,1)} %table_ref.1), custom_call_target="tpu_custom_call" | custom-call | tf_op jit(solution)/shard_map/pallas_call | solution.py:365
  49.5 0.0 copy-done.6
  49.5 0.2 copy.12
  49.7 0.1 pad.4.cell_ref
  49.8 0.0 copy-start.1
  49.8 1.3 copy-done.1
  51.1 0.0 copy-start.2
  51.2 1.1 copy-done.2
  52.3 0.0 copy-start.5
  52.3 76.7 %shard_map.105 = (bf16[8,64,128]{2,1,0:T(8,128)(2,1)S(1)}, f32[8,128]{1,0:T(8,128)S(1)}) custom-call(s32[2]{0:T(128)S(1)} %pad_add_fusion.where_ref, f32[4,12]{1,0:T(4,128)S(1)} %maximum_maximum_fusion.mode_ref, bf16[8,80,1024]{2,1,0:T(8,128)(2,1)S(1)} %copy-done.1, bf16[512,768]{1,0:T(8,128)(2,1)S(1)} %bitcast.9, bf16[512,16]{1,0:T(8,128)(2,1)S(1)} %pad.4.cell_ref), custom_call_target="tpu_custom_call" | custom-call | tf_op jit(solution)/shard_map/pallas_call | solution.py:377
  129.0 0.0 copy-start.3
  129.0 0.6 copy-done.3
  129.6 0.0 copy-start.4
  129.6 0.6 copy-done.4
  130.2 25.3 %shard_map.106 = (f32[64,128]{1,0:T(8,128)}, f32[8,8,128]{2,1,0:T(8,128)}) custom-call(bf16[8,64,128]{2,1,0:T(8,128)(2,1)} %copy-done.3, f32[8,128]{1,0:T(8,128)} %copy-done.4), custom_call_target="tpu_custom_call" | custom-call | tf_op jit(solution)/shard_map/pallas_call | solution.py:403
  155.5 0.8 broadcast_multiply_fusion
  156.3 0.6 mul.30
  156.9 0.8 slice.3
  157.7 0.0 copy-done.5
  157.7 0.6 multiply_multiply_fusion
  (5 shorter events, 0.0 us)
Async XLA Ops:
  0.6 0.8 copy-start
  0.6 48.9 %copy-start.6 = (s32[512,3]{0,1:T(4,128)S(1)}, s32[512,3]{0,1:T(4,128)}, u32[]{:S(2)}) copy-start(s32[512,3]{0,1:T(4,128)} %param.10) | copy-start | bytes 18436
  49.8 1.3 copy-start.1
  51.1 1.1 copy-start.2
  52.3 105.4 %copy-start.5 = (bf16[8,12]{1,0:T(8,128)(2,1)S(1)}, bf16[8,12]{1,0:T(8,128)(2,1)}, u32[]{:S(2)}) copy-start(bf16[8,12]{1,0:T(8,128)(2,1)} %param.15) | copy-start | bytes 580
  129.0 0.6 copy-start.3
  129.6 0.6 copy-start.4

commit v3 on v0

v3 whole, which is shorter than its diff:
```python
import math

import jax
import jax.numpy as jnp
from jax import lax
from jax.experimental import pallas as pl
from jax.experimental.pallas import tpu as pltpu
from jax.sharding import PartitionSpec as P

NB = 8
NM = 12
ETA = 0.05
TOGETHER = 2
ROWS = 80
MESH = pl.DeviceIdType.MESH
SIN = (6.28318516, -41.3416549, 81.6009982, -76.5496568, 39.5358137)


def fused(
    mode_ref,
    shift_ref,
    u_ref,
    aux_ref,
    table_ref,
    cell_ref,
    energy_ref,
    widths_ref,
    u_all,
    aux_all,
    part,
    flat,
    turned_flat,
    table,
    phase,
    interp,
    near,
    far,
    window,
    level,
    sums,
    acc,
    sigma,
    width,
    got,
    got_w,
    send_aux,
    recv_aux,
    send_part,
    recv_part,
    send_u,
    recv_u,
    send_s,
    recv_s,
    send_w,
    recv_w,
    own_sems,
):
    count = u_all.shape[0]
    q_local = table_ref.shape[0]
    cells = table_ref.shape[1]
    cores = got.shape[0] // q_local
    per_q = count // q_local
    me, core = lax.axis_index("ka"), lax.axis_index("pb")
    q_mine, range_mine = me // per_q, lax.rem(me, per_q)
    slot_mine = core * q_local + q_mine
    everyone = count * cores
    mine = me * cores + core
    barrier = pltpu.get_barrier_semaphore()

    def greet(step, carry):
        other = lax.rem(mine + step, everyone)
        pl.semaphore_signal(
            barrier, inc=1, device_id={"ka": other // cores, "pb": lax.rem(other, cores)}, device_id_type=MESH
        )
        return carry

    lax.fori_loop(1, everyone, greet, 0)
    aux_all[me] = aux_ref[...]
    u_all[me] = u_ref[...]
    own_part = pltpu.make_async_copy(table_ref.at[q_mine], part.at[me], own_sems.at[0])
    own_part.start()
    acc[...] = jnp.zeros_like(acc)
    pl.semaphore_wait(barrier, everyone - 1)

    def to_peer(step, source, target, send, recv, sender):
        return pltpu.make_async_remote_copy(
            src_ref=source,
            dst_ref=target.at[sender],
            send_sem=send.at[step],
            recv_sem=recv.at[sender],
            device_id={"ka": lax.rem(me + step, count)},
            device_id_type=MESH,
        )

    def aux_copy(step, sender):
        return to_peer(step, aux_ref, aux_all, send_aux, recv_aux, sender)

    def part_copy(step, sender):
        return to_peer(step, table_ref.at[lax.rem(me + step, count) // per_q], part, send_part, recv_part, sender)

    def u_copy(step, sender):
        return to_peer(step, u_ref, u_all, send_u, recv_u, sender)

    def width_copy(step, sender):
        return to_peer(step, width, got_w, send_w, recv_w, sender)

    def over_peers(act):
        def body(step, carry):
            act(step, lax.rem(me + step, count))
            return carry

        lax.fori_loop(1, count, body, 0)

    over_peers(lambda step, peer: aux_copy(step, me).start())
    over_peers(lambda step, peer: part_copy(step, me).start())
    over_peers(lambda step, peer: aux_copy(step, peer).wait_recv())

    def phases(b, carry):
        product = jnp.dot(cell_ref[...], aux_all[range_mine * q_local + b], preferred_element_type=jnp.float32)
        turn = product * 0.01
        turn = jnp.abs(turn - jnp.floor(turn + 0.5))
        angle = 0.25 - turn
        square = angle * angle
        value = SIN[4]
        for coefficient in (SIN[3], SIN[2], SIN[1], SIN[0]):
            value = value * square + coefficient
        phase[b] = (value * angle).astype(jnp.bfloat16)
        return carry

    lax.fori_loop(0, q_local, phases, 0)
    own_part.wait()
    over_peers(lambda step, peer: aux_copy(step, me).wait_send())
    over_peers(lambda step, peer: part_copy(step, me).wait_send())
    over_peers(lambda step, peer: u_copy(step, me).start())
    over_peers(lambda step, peer: part_copy(step, peer).wait_recv())

    def flatten(sender, carry):
        flat[pl.ds(pl.multiple_of(sender * cells, cells), cells), :] = part[sender].astype(jnp.float32)
        return carry

    lax.fori_loop(0, count, flatten, 0)
    whole = jnp.transpose(flat[...])
    for j in range(turned_flat.shape[0]):
        turned_flat[j] = whole[:, j * 128 : (j + 1) * 128]
    for v in range(NM):
        for j in range(turned_flat.shape[0]):
            rows = [turned_flat[j, pl.ds(v * 64 + b, 8, stride=8), :] for b in range(NB)]
            table[v * 64 : v * 64 + 64, j * 128 : (j + 1) * 128] = jnp.concatenate(rows, axis=0).astype(jnp.bfloat16)

    def interpolate(b, carry):
        for third in range(3):
            folded = jnp.dot(table[third * 256 : third * 256 + 256, :], phase[b], preferred_element_type=jnp.float32)
            for c in range(8):
                interp[b, pl.ds(third * 2048 + c, 256, stride=8), :] = folded[:, c * 128 : (c + 1) * 128]
        return carry

    lax.fori_loop(0, q_local, interpolate, 0)
    over_peers(lambda step, peer: u_copy(step, me).wait_send())
    over_peers(lambda step, peer: u_copy(step, peer).wait_recv())

    inv_t = mode_ref[3, 0]

    def sigma_copy(index, slot):
        b, to_core = index // cores, lax.rem(index, cores)
        return pltpu.make_async_remote_copy(
            src_ref=sigma.at[b],
            dst_ref=got.at[slot],
            send_sem=send_s.at[index],
            recv_sem=recv_s.at[slot],
            device_id={"ka": range_mine * q_local + b, "pb": to_core},
            device_id_type=MESH,
        )

    def group(ref, start):
        return ref[pl.ds(pl.multiple_of(start, 64), 64), :].reshape(8, 8, 128)

    def fermi(energy):
        return 1.0 / (1.0 + jnp.exp(energy * inv_t))

    def one_block(step, carry):
        b = lax.rem(step + me, q_local)
        block = range_mine * q_local + b
        for c in range(8):
            near[pl.ds(c, 64, stride=8), :] = u_all[block, :, c * 128 : (c + 1) * 128].astype(jnp.float32)
            near[pl.ds(512 + c, 16, stride=8), :] = aux_all[block, :, c * 128 : (c + 1) * 128].astype(jnp.float32)
        for c in range(16):
            lane = pl.ds(c % 8 * 128, 128)

            def chunk(j):
                index = lax.rem(block + c // 8 + j, count)
                rows = aux_all[index, :, lane].astype(jnp.float32)[0:8]
                return jnp.concatenate([u_all[index, :, lane].astype(jnp.float32), rows], axis=0)

            def pick(j, kept):
                wanted = shift_ref[0:1, :] == j.astype(jnp.float32)
                return jnp.where(wanted, chunk(j), kept)

            window[c] = lax.fori_loop(1, count, pick, chunk(0), unroll=count <= 8)
        parts = [window[c] for c in range(12)]
        four = shift_ref[1:2, :] > 0.5
        parts = [jnp.where(four, window[c + 4], parts[c]) for c in range(12)]
        two = shift_ref[2:3, :] > 0.5
        parts = [jnp.where(two, parts[c + 2], parts[c]) for c in range(10)]
        one = shift_ref[3:4, :] > 0.5
        for c in range(9):
            window[c] = jnp.where(one, parts[c + 1], parts[c])
        lanes = lax.broadcasted_iota(jnp.int32, (72, 128), 1).astype(jnp.float32)

        def turned(c):
            rows = window[c]
            for bit in range(7):
                rows = jnp.where(shift_ref[4 + bit : 5 + bit, :] > 0.5, pltpu.roll(rows, 128 - 2**bit, 1), rows)
            return rows

        here = turned(0)
        for c in range(8):
            after = turned(c + 1)
            far[pl.ds(c, 72, stride=8), :] = jnp.where(lanes < 128.0 - shift_ref[11:12, :], here, after)
            here = after

        e_m = group(far, 512)
        f_m = fermi(e_m)
        tally = near[600:608, :]

        def over_n(n, inner_carry):
            e_n = near[pl.ds(pl.multiple_of(512 + n * 8, 8), 8), :]
            f_n = fermi(e_n)
            mask = jnp.where(n.astype(jnp.float32) < tally, 1.0, 0.0)
            gap = e_n[None] - e_m
            level[0] = gap * gap + ETA * ETA
            level[1] = gap + gap
            level[2] = mask[None] * (f_n[None] - f_m)
            level[3] = (1.0 - 2.0 * f_m) * (gap + gap)
            u_n = [near[pl.ds(pl.multiple_of(i * 64 + n * 8, 8), 8), :] for i in range(NB)]

            def over_v(pair, total):
                modes = [pair * TOGETHER + i for i in range(TOGETHER)]
                inner = []
                for v in modes:
                    term = None
                    for i in range(NB):
                        start = pl.multiple_of(v * 512 + i * 64, 64)
                        more = interp[b, pl.ds(start, 64), :].reshape(8, 8, 128) * u_n[i][None]
                        term = more if term is None else term + more
                    inner.append(term)
                rotated = [None] * TOGETHER
                for a in range(NB):
                    u_a = group(far, a * 64)
                    for i in range(TOGETHER):
                        more = u_a * inner[i][a][None]
                        rotated[i] = more if a == 0 else rotated[i] + more
                for i, v in enumerate(modes):
                    w = mode_ref[0, v]
                    even = level[0] + mode_ref[1, v]
                    odd = level[1] * w
                    low = even - odd
                    scaled = rotated[i] * rotated[i] * pl.reciprocal(low * (even + odd), approx=True)
                    total = total + jnp.sum(scaled * (mode_ref[2, v] * even + w * level[3]), axis=0)
                    spot = pl.ds(pl.multiple_of(v * 8, 8), 8)
                    acc[spot, :] = acc[spot, :] + jnp.sum(level[2] * (low * scaled), axis=0)
                return total

            total = lax.fori_loop(0, NM // TOGETHER, over_v, jnp.zeros((8, 128), jnp.float32))
            sums[pl.ds(pl.multiple_of(n * 8, 8), 8), :] = mask * total
            return inner_carry

        lax.fori_loop(0, NB, over_n, 0)
        sigma[b] = sums[...].astype(jnp.bfloat16)
        for to_core in range(cores):

            @pl.when(block * cores + to_core != mine)
            def _():
                sigma_copy(b * cores + to_core, slot_mine).start()

            @pl.when(block * cores + to_core == mine)
            def _():
                got[slot_mine] = sigma[b]

        return carry

    lax.fori_loop(0, q_local, one_block, 0)
    lane = lax.broadcasted_iota(jnp.int32, (8, 128), 1)
    out = jnp.zeros((8, 128), jnp.float32)
    for v in range(NM):
        out = out + jnp.where(lane == v, jnp.sum(acc[v * 8 : v * 8 + 8, :]), 0.0)
    width[...] = out
    got_w[me] = out
    over_peers(lambda step, peer: width_copy(step, me).start())

    def finish_s(index, carry):
        target = (range_mine * q_local + index // cores) * cores + lax.rem(index, cores)

        @pl.when(target != mine)
        def _():
            sigma_copy(index, slot_mine).wait_send()

        from_core, from_q = index // q_local, lax.rem(index, q_local)
        source = (from_q * per_q + me // q_local) * cores + from_core

        @pl.when(source != mine)
        def _():
            sigma_copy(index, index).wait_recv()

        return carry

    lax.fori_loop(0, q_local * cores, finish_s, 0)
    total = got[0].astype(jnp.float32)
    for slot in range(1, q_local * cores):
        total = total + got[slot].astype(jnp.float32)
    sums[...] = total * (ETA / math.pi / (q_local * cores * NM))
    for c in range(8):
        energy_ref[:, c * 128 : (c + 1) * 128] = sums[pl.ds(c, 8, stride=8), :]
    over_peers(lambda step, peer: width_copy(step, me).wait_send())
    over_peers(lambda step, peer: width_copy(step, peer).wait_recv())
    for q in range(q_local):
        total = got_w[q * per_q]
        for part_of in range(1, per_q):
            total = total + got_w[q * per_q + part_of]
        widths_ref[q, :, :] = total


def on_device(
    momentum_mesh_positions,
    bravais_translation_list,
    localized_matrix_element_table,
    unitary_band_mixer,
    quasiparticle_level_offsets,
    displaced_momentum_slot,
    vibration_mode_pulsations,
    occupied_band_tally,
    heat_bath_scale,
):
    kcount = momentum_mesh_positions.shape[1]
    q_local, cells, feat = localized_matrix_element_table.shape
    count, cores = lax.axis_size("ka"), lax.axis_size("pb")
    k_total = kcount * count
    per_q = count // q_local
    me = lax.axis_index("ka")
    tau = heat_bath_scale[0]
    aux = jnp.concatenate(
        [
            quasiparticle_level_offsets,
            momentum_mesh_positions.astype(jnp.bfloat16),
            jnp.broadcast_to(occupied_band_tally.astype(jnp.bfloat16)[:, None], (1, kcount)),
            jnp.zeros((4, kcount), jnp.bfloat16),
        ],
        axis=0,
    )
    q_mine = me // per_q
    slot = lax.dynamic_slice(displaced_momentum_slot, (q_mine, 0), (1, 1))[0, 0]
    shift = jnp.mod(slot - me * kcount, k_total)
    freq_own = vibration_mode_pulsations.astype(jnp.float32)
    freq = lax.dynamic_slice_in_dim(freq_own, q_mine, 1, 0)[0]
    twice = 2.0 / (jnp.exp(freq / tau) - 1.0) + 1.0
    modes = jnp.stack([freq, freq * freq, twice, jnp.broadcast_to(1.0 / tau, (NM,))])
    cell_rows = jnp.pad(bravais_translation_list.astype(jnp.bfloat16), ((0, 0), (8, 5)))

    anywhere = pl.BlockSpec(memory_space=pl.ANY)
    in_vmem = pl.BlockSpec(memory_space=pltpu.VMEM)
    in_smem = pl.BlockSpec(memory_space=pltpu.SMEM)
    inside = shift % kcount
    steps = [shift // kcount, inside // 512, inside // 256 % 2, inside // 128 % 2]
    steps += [inside // 2**bit % 2 for bit in range(7)] + [inside % 128]
    steps = jnp.broadcast_to(jnp.stack(steps + [shift] * 4).astype(jnp.float32)[:, None], (16, 128))
    peers = pltpu.SemaphoreType.DMA((count,))
    slots = pltpu.SemaphoreType.DMA((cores * q_local,))
    self_energy, widths = pl.pallas_call(
        fused,
        out_shape=(
            jax.ShapeDtypeStruct((NB, kcount), jnp.float32),
            jax.ShapeDtypeStruct((q_local, 8, 128), jnp.float32),
        ),
        in_specs=[in_smem, in_vmem, in_vmem, in_vmem, anywhere, in_vmem],
        out_specs=(in_vmem, in_vmem),
        scratch_shapes=[
            pltpu.VMEM((count, 64, kcount), jnp.bfloat16),
            pltpu.VMEM((count, 16, kcount), jnp.bfloat16),
            pltpu.VMEM((count, cells, feat), jnp.bfloat16),
            pltpu.VMEM((count * cells, feat), jnp.float32),
            pltpu.VMEM((count * cells // 128, feat, 128), jnp.float32),
            pltpu.VMEM((feat, count * cells), jnp.bfloat16),
            pltpu.VMEM((q_local, count * cells, kcount), jnp.bfloat16),
            pltpu.VMEM((q_local, feat * 8, 128), jnp.float32),
            pltpu.VMEM((ROWS * 8, 128), jnp.float32),
            pltpu.VMEM((ROWS * 8, 128), jnp.float32),
            pltpu.VMEM((16, 72, 128), jnp.float32),
            pltpu.VMEM((4, NB, 8, 128), jnp.float32),
            pltpu.VMEM((NB * 8, 128), jnp.float32),
            pltpu.VMEM((NM * 8, 128), jnp.float32),
            pltpu.VMEM((q_local, NB * 8, 128), jnp.bfloat16),
            pltpu.VMEM((8, 128), jnp.float32),
            pltpu.VMEM((cores * q_local, NB * 8, 128), jnp.bfloat16),
            pltpu.VMEM((count, 8, 128), jnp.float32),
            peers,
            peers,
            peers,
            peers,
            peers,
            peers,
            slots,
            slots,
            peers,
            peers,
            pltpu.SemaphoreType.DMA((1,)),
        ],
        compiler_params=pltpu.CompilerParams(
            collective_id=0, has_side_effects=True, vmem_limit_bytes=60 * 1024 * 1024
        ),
    )(
        modes,
        steps,
        unitary_band_mixer,
        aux,
        localized_matrix_element_table,
        cell_rows,
    )
    linewidth = widths[:, 0, :NM] * freq_own * (2.0 * math.pi * ETA / math.pi / k_total)
    return (self_energy, linewidth)


def solution(mesh):
    return jax.shard_map(
        on_device,
        mesh=mesh,
        in_specs=(
            P(None, "ka"),
            P(),
            P(("grp", "pb"), "ka", None),
            P(None, ("grp", "ka")),
            P(None, ("grp", "ka")),
            P(("grp", "pb"), "ka"),
            P(("grp", "pb"), None),
            P(("grp", "ka")),
            P("grp"),
        ),
        out_specs=(P(None, ("grp", "ka")), P(("grp", "pb"), None)),
        check_vma=False,
    )
```

time: 743 us -> 123 us (0.17)
  local copies, waits for them, and re-layouts: 266 us -> 5.36 us
  waiting for transfers between devices: 180 us -> 0 us
  other arithmetic: 155 us -> 1.98 us
  Pallas kernels: 0 us -> 113 us
  blocking collectives: 99.4 us -> 0 us
  matrix products: 17.7 us -> 0 us
  between operations: 15.2 us -> 3.03 us
    all_gather x3 -> x0, waiting for transfers between devices: 179 us -> none  [the longest x1 133 us: on_device(): lax.all_gather(coupling_all, 'ka', axis=1, tiled=True)]
    pallas_call x0 -> x1, Pallas kernels: none -> 113 us  [on_device(): pl.pallas_call(fused, out_shape=(jax.ShapeDtypeStruct((NB, kcount), jnp.f...]
    gather x48 -> x0, local copies, waits for them, and re-layouts: 94.3 us -> none  [the longest x32 47.8 us: advance(): e_far = jnp.take(en_all, kq_rows, axis=1).astype(jnp.float32)]
    slice x162 -> x1, local copies, waits for them, and re-layouts: 85.1 us -> 0.76 us  [on_device(): widths[:, 0, :NM] * freq_own * (2.0 * math.pi * ETA / math.pi / k_total)]
    all_gather x4 -> x0, blocking collectives: 67.7 us -> none  [the longest x1 62.1 us: on_device(): lax.all_gather(quasiparticle_level_offsets, 'ka', axis=1, tiled=True)]
    reduce_sum x32 -> x0, other arithmetic: 51.4 us -> none  [the longest x16 30 us: advance(): self_term = jnp.sum(squared * kpoint_weight, axis=(0, 1))]
    mul x32 -> x2, other arithmetic: 32.6 us -> 0.61 us  [the longest x1 0.6 us: on_device(): widths[:, 0, :NM] * freq_own * (2.0 * math.pi * ETA / math.pi / k_total)]
    psum x1 -> x0, blocking collectives: 31.7 us -> none  [on_device(): widths = lax.psum(widths, ('ka', 'pb'))]
  transfers between devices with their start and end apart: 3 -> 0, of which waited for: 3 -> 0; matrix products, arithmetic and copies ran while one was open for 3% -> 0% of each run, Pallas kernels for 0% -> 0%
where the time goes in v3:
time: 123 us
  Pallas kernels  113 us (92%)
  local copies, waits for them, and re-layouts  5.36 us (4%)
  between operations  3.03 us (2%)
  other arithmetic  1.98 us (2%)
    pallas_call x1, Pallas kernels, on_device(): pl.pallas_call(fused, out_shape=(jax.ShapeDtypeStruct((NB, kcount), jnp.f...  113 us

profile of v3, /device:TPU:0, one launch (start us, length us, event | category | flops | bytes accessed | tf_op | source)
XLA Modules:
  0.0 123.1 jit_solution(15650241389264987018)
XLA Ops:
  0.6 0.0 copy-start
  0.6 0.7 copy-done
  1.4 0.5 constant_dynamic-slice_fusion
  2.9 0.1 stack.64
  3.0 0.0 copy-start.3
  3.0 0.7 broadcast_in_dim.8.shift_ref
  3.6 0.0 copy-done.3
  4.3 0.0 copy-start.4
  4.4 0.1 pad.12.clone
  4.5 0.7 maximum_maximum_fusion.1.mode_ref
  5.1 0.0 copy-done.4
  5.1 0.2 copy.12
  5.3 0.0 copy-start.2
  5.3 0.8 pad.4.cell_ref
  6.1 0.0 copy-done.2
  6.1 0.0 copy-start.1
  6.8 0.1 pad.7.clone
  6.9 0.1 pad.8.clone
  6.9 0.0 copy-done.1
  6.9 0.7 maximum_maximum_fusion.aux_ref
  7.6 112.7 %shard_map.104 = (f32[8,1024]{1,0:T(8,128)}, f32[8,8,128]{2,1,0:T(8,128)}) custom-call(f32[4,12]{1,0:T(4,128)} %maximum_maximum_fusion.1.mode_ref, f32[16,128]{1,0:T(8,128)} %broadcast_in_dim.8.shift_ref, bf16[64,1024]{1,0:T(8,128)(2,1)} %u_ref.1, bf16[16,1024]{1,0:T(8,128)(2,1)} %maximum_maximum_fusion.aux_ref, bf16[8,64,768]{2,1,0:T(8,128)(2,1)} %table_ref.1, ...), custom_call_target="tpu_custom_call" | custom-call | tf_op jit(solution)/shard_map/pallas_call | solution.py:367
  120.3 0.8 slice.3
  121.1 0.6 multiply_multiply_fusion
  121.7 1.4 %copy.16 = f32[8,1024]{1,0:T(8,128)} copy(f32[8,1024]{1,0:T(8,128)} %get-tuple-element.10) | data formatting | bytes 65536
  (7 shorter events, 0.0 us)
Async XLA Ops:
  0.6 0.8 copy-start
  3.0 0.7 copy-start.3
  4.3 0.8 copy-start.4
  5.3 0.8 copy-start.2
  6.1 0.8 copy-start.1

commit v4 on v3

--- a/solution.py
+++ b/solution.py
@@ -10,7 +10,7 @@
 NB = 8
 NM = 12
 ETA = 0.05
-TOGETHER = 2
+TOGETHER = 3
 ROWS = 80
 MESH = pl.DeviceIdType.MESH
 SIN = (6.28318516, -41.3416549, 81.6009982, -76.5496568, 39.5358137)
@@ -23,6 +23,7 @@
     aux_ref,
     table_ref,
     cell_ref,
+    freq_ref,
     energy_ref,
     widths_ref,
     u_all,
@@ -49,6 +50,8 @@
     recv_part,
     send_u,
     recv_u,
+    send_f,
+    recv_f,
     send_s,
     recv_s,
     send_w,
@@ -98,8 +101,29 @@
     def part_copy(step, sender):
         return to_peer(step, table_ref.at[lax.rem(me + step, count) // per_q], part, send_part, recv_part, sender)
 
+    half = u_ref.shape[1] // cores
+
     def u_copy(step, sender):
-        return to_peer(step, u_ref, u_all, send_u, recv_u, sender)
+        columns = pl.ds(pl.multiple_of(core * half, half), half)
+        return pltpu.make_async_remote_copy(
+            src_ref=u_ref.at[:, columns],
+            dst_ref=u_all.at[sender, :, columns],
+            send_sem=send_u.at[step],
+            recv_sem=recv_u.at[sender],
+            device_id={"ka": lax.rem(me + step, count)},
+            device_id_type=MESH,
+        )
+
+    def pass_on(sender, from_core):
+        columns = pl.ds(pl.multiple_of(from_core * half, half), half)
+        return pltpu.make_async_remote_copy(
+            src_ref=u_all.at[sender, :, columns],
+            dst_ref=u_all.at[sender, :, columns],
+            send_sem=send_f.at[sender],
+            recv_sem=recv_f.at[sender],
+            device_id={"pb": 1 - core},
+            device_id_type=MESH,
+        )
 
     def width_copy(step, sender):
         return to_peer(step, width, got_w, send_w, recv_w, sender)
@@ -148,15 +172,25 @@
             table[v * 64 : v * 64 + 64, j * 128 : (j + 1) * 128] = jnp.concatenate(rows, axis=0).astype(jnp.bfloat16)
 
     def interpolate(b, carry):
-        for third in range(3):
-            folded = jnp.dot(table[third * 256 : third * 256 + 256, :], phase[b], preferred_element_type=jnp.float32)
-            for c in range(8):
-                interp[b, pl.ds(third * 2048 + c, 256, stride=8), :] = folded[:, c * 128 : (c + 1) * 128]
+        folded = jnp.dot(table[...], phase[b], preferred_element_type=jnp.float32)
+        for c in range(8):
+            interp[b, pl.ds(c, 64 * NM, stride=8), :] = folded[:, c * 128 : (c + 1) * 128]
+
+        def relay(step, inner_carry):
+            peer = lax.rem(me + step, count)
+            u_copy(step, peer).wait_recv()
+            pass_on(peer, core).start()
+            return inner_carry
+
+        batch = count // (q_local // 2)
+        late = b - q_local // 2
+        lax.fori_loop(jnp.maximum(late * batch, 1), (late + 1) * batch, relay, 0)
         return carry
 
     lax.fori_loop(0, q_local, interpolate, 0)
     over_peers(lambda step, peer: u_copy(step, me).wait_send())
-    over_peers(lambda step, peer: u_copy(step, peer).wait_recv())
+    over_peers(lambda step, peer: pass_on(peer, core).wait_send())
+    over_peers(lambda step, peer: pass_on(peer, 1 - core).wait_recv())
 
     inv_t = mode_ref[3, 0]
 
@@ -316,7 +350,7 @@
         total = got_w[q * per_q]
         for part_of in range(1, per_q):
             total = total + got_w[q * per_q + part_of]
-        widths_ref[q, :, :] = total
+        widths_ref[q : q + 1, :] = total[0:1, :NM] * freq_ref[q : q + 1, :] * (2.0 * ETA / (count * u_ref.shape[1]))
 
 
 def on_device(
@@ -364,13 +398,13 @@
     steps = jnp.broadcast_to(jnp.stack(steps + [shift] * 4).astype(jnp.float32)[:, None], (16, 128))
     peers = pltpu.SemaphoreType.DMA((count,))
     slots = pltpu.SemaphoreType.DMA((cores * q_local,))
-    self_energy, widths = pl.pallas_call(
+    self_energy, linewidth = pl.pallas_call(
         fused,
         out_shape=(
             jax.ShapeDtypeStruct((NB, kcount), jnp.float32),
-            jax.ShapeDtypeStruct((q_local, 8, 128), jnp.float32),
+            jax.ShapeDtypeStruct((q_local, NM), jnp.float32),
         ),
-        in_specs=[in_smem, in_vmem, in_vmem, in_vmem, anywhere, in_vmem],
+        in_specs=[in_smem, in_vmem, in_vmem, in_vmem, anywhere, in_vmem, in_vmem],
         out_specs=(in_vmem, in_vmem),
         scratch_shapes=[
             pltpu.VMEM((count, 64, kcount), jnp.bfloat16),
@@ -397,6 +431,8 @@
             peers,
             peers,
             peers,
+            peers,
+            peers,
             slots,
             slots,
             peers,
@@ -413,8 +449,8 @@
         aux,
         localized_matrix_element_table,
         cell_rows,
+        freq_own,
     )
-    linewidth = widths[:, 0, :NM] * freq_own * (2.0 * math.pi * ETA / math.pi / k_total)
     return (self_energy, linewidth)
 
 

time: 123 us -> 114 us (0.927)
  Pallas kernels: 113 us -> 104 us
    pallas_call x1, Pallas kernels: 113 us -> 104 us  [on_device(): pl.pallas_call(fused, out_shape=(jax.ShapeDtypeStruct((NB, kcount), jnp.f...]
    unnamed x11 -> x16, local copies, waits for them, and re-layouts: 2.16 us -> 2.76 us
where the time goes in v4:
time: 114 us
  Pallas kernels  104 us (91%)
  local copies, waits for them, and re-layouts  5.2 us (5%)
  between operations  3.04 us (3%)
  other arithmetic  1.39 us (1%)
    pallas_call x1, Pallas kernels, on_device(): pl.pallas_call(fused, out_shape=(jax.ShapeDtypeStruct((NB, kcount), jnp.f...  104 us
    unnamed x16, local copies, waits for them, and re-layouts  2.76 us

profile of v4, /device:TPU:0, one launch (start us, length us, event | category | flops | bytes accessed | tf_op | source)
XLA Modules:
  0.0 113.6 jit_solution(13662617889302034837)
XLA Ops:
  0.6 0.0 copy-start
  0.6 0.7 copy-done
  1.4 0.5 constant_dynamic-slice_fusion
  2.9 0.1 stack.64
  3.0 0.0 copy-start.6
  3.0 0.7 broadcast_in_dim.8.shift_ref
  3.6 0.0 copy-done.6
  3.7 0.0 copy-start.1
  4.3 0.0 copy-start.4
  4.4 0.0 copy-done.1
  4.4 0.1 pad.12.clone
  4.5 0.7 maximum_maximum_fusion.1.mode_ref
  5.1 0.0 copy-done.4
  5.2 0.2 copy.12
  5.3 0.0 copy-start.3
  5.4 0.8 pad.4.cell_ref
  6.1 0.0 copy-done.3
  6.1 0.0 copy-start.2
  6.8 0.1 pad.7.clone
  6.9 0.1 pad.8.clone
  6.9 0.0 copy-done.2
  6.9 0.7 maximum_maximum_fusion.aux_ref
  7.6 103.9 %shard_map.104 = (f32[8,1024]{1,0:T(8,128)}, f32[8,12]{1,0:T(8,128)}) custom-call(f32[4,12]{1,0:T(4,128)} %maximum_maximum_fusion.1.mode_ref, f32[16,128]{1,0:T(8,128)} %broadcast_in_dim.8.shift_ref, bf16[64,1024]{1,0:T(8,128)(2,1)} %u_ref.1, bf16[16,1024]{1,0:T(8,128)(2,1)} %maximum_maximum_fusion.aux_ref, bf16[8,64,768]{2,1,0:T(8,128)(2,1)} %table_ref.1, ...), custom_call_target="tpu_custom_call" | custom-call | tf_op jit(solution)/shard_map/pallas_call | solution.py:401
  111.6 0.0 copy-start.5
  111.6 1.4 %copy.17 = f32[8,1024]{1,0:T(8,128)} copy(f32[8,1024]{1,0:T(8,128)} %get-tuple-element.6) | data formatting | bytes 65536
  113.0 0.0 copy-done.5
  113.0 0.6 copy.18
  (7 shorter events, 0.0 us)
Async XLA Ops:
  0.6 0.8 copy-start
  3.0 0.7 copy-start.6
  3.7 0.7 copy-start.1
  4.3 0.8 copy-start.4
  5.3 0.8 copy-start.3
  6.1 0.8 copy-start.2
  111.6 1.4 %copy-start.5 = (f32[8,12]{1,0:T(8,128)S(1)}, f32[8,12]{1,0:T(8,128)}, u32[]{:S(2)}) copy-start(f32[8,12]{1,0:T(8,128)} %get-tuple-element.7) | copy-start | bytes 1156

commit v5 on v4

--- a/solution.py
+++ b/solution.py
@@ -36,6 +36,7 @@
     interp,
     near,
     far,
+    raw,
     window,
     level,
     sums,
@@ -211,28 +212,34 @@
     def fermi(energy):
         return 1.0 / (1.0 + jnp.exp(energy * inv_t))
 
-    def one_block(step, carry):
-        b = lax.rem(step + me, q_local)
+    def fetch(block):
+        for c in range(8):
+            lane = pl.ds(c * 128, 128)
+
+            def chunk(j):
+                index = lax.rem(block + j, count)
+                rows = aux_all[index, :, lane].astype(jnp.float32)[0:8]
+                return jnp.concatenate([u_all[index, :, lane].astype(jnp.float32), rows], axis=0)
+
+            def pick(j, kept):
+                wanted = shift_ref[0:1, :] == j.astype(jnp.float32)
+                return jnp.where(wanted, chunk(j), kept)
+
+            raw[8 + c] = lax.fori_loop(1, count, pick, chunk(0), unroll=count <= 8)
+
+    fetch(range_mine * q_local)
+
+    def one_block(b, carry):
         block = range_mine * q_local + b
         for c in range(8):
             near[pl.ds(c, 64, stride=8), :] = u_all[block, :, c * 128 : (c + 1) * 128].astype(jnp.float32)
             near[pl.ds(512 + c, 16, stride=8), :] = aux_all[block, :, c * 128 : (c + 1) * 128].astype(jnp.float32)
-        for c in range(16):
-            lane = pl.ds(c % 8 * 128, 128)
-
-            def chunk(j):
-                index = lax.rem(block + c // 8 + j, count)
-                rows = aux_all[index, :, lane].astype(jnp.float32)[0:8]
-                return jnp.concatenate([u_all[index, :, lane].astype(jnp.float32), rows], axis=0)
-
-            def pick(j, kept):
-                wanted = shift_ref[0:1, :] == j.astype(jnp.float32)
-                return jnp.where(wanted, chunk(j), kept)
-
-            window[c] = lax.fori_loop(1, count, pick, chunk(0), unroll=count <= 8)
-        parts = [window[c] for c in range(12)]
+        for c in range(8):
+            raw[c] = raw[8 + c]
+        fetch(block + 1)
+        parts = [raw[c] for c in range(12)]
         four = shift_ref[1:2, :] > 0.5
-        parts = [jnp.where(four, window[c + 4], parts[c]) for c in range(12)]
+        parts = [jnp.where(four, raw[c + 4], parts[c]) for c in range(12)]
         two = shift_ref[2:3, :] > 0.5
         parts = [jnp.where(two, parts[c + 2], parts[c]) for c in range(10)]
         one = shift_ref[3:4, :] > 0.5
@@ -418,6 +425,7 @@
             pltpu.VMEM((ROWS * 8, 128), jnp.float32),
             pltpu.VMEM((ROWS * 8, 128), jnp.float32),
             pltpu.VMEM((16, 72, 128), jnp.float32),
+            pltpu.VMEM((9, 72, 128), jnp.float32),
             pltpu.VMEM((4, NB, 8, 128), jnp.float32),
             pltpu.VMEM((NB * 8, 128), jnp.float32),
             pltpu.VMEM((NM * 8, 128), jnp.float32),

time: 114 us -> 114 us (level)
  no operation moved by 1% of the time
where the time goes in v5:
time: 114 us
  Pallas kernels  104 us (91%)
  local copies, waits for them, and re-layouts  5.2 us (5%)
  between operations  3.04 us (3%)
  other arithmetic  1.39 us (1%)
    pallas_call x1, Pallas kernels, on_device(): pl.pallas_call(fused, out_shape=(jax.ShapeDtypeStruct((NB, kcount), jnp.f...  104 us
    unnamed x16, local copies, waits for them, and re-layouts  2.76 us

profile of v5, /device:TPU:0, one launch (start us, length us, event | category | flops | bytes accessed | tf_op | source)
XLA Modules:
  0.0 114.1 jit_solution(3797699291578324117)
XLA Ops:
  0.6 0.0 copy-start
  0.6 0.7 copy-done
  1.4 0.5 constant_dynamic-slice_fusion
  2.9 0.1 stack.64
  3.0 0.0 copy-start.6
  3.0 0.7 broadcast_in_dim.8.shift_ref
  3.6 0.0 copy-done.6
  3.7 0.0 copy-start.1
  4.3 0.0 copy-start.4
  4.4 0.0 copy-done.1
  4.4 0.1 pad.12.clone
  4.5 0.7 maximum_maximum_fusion.1.mode_ref
  5.1 0.0 copy-done.4
  5.2 0.2 copy.12
  5.3 0.0 copy-start.3
  5.4 0.8 pad.4.cell_ref
  6.1 0.0 copy-done.3
  6.1 0.0 copy-start.2
  6.8 0.1 pad.7.clone
  6.9 0.1 pad.8.clone
  6.9 0.0 copy-done.2
  6.9 0.7 maximum_maximum_fusion.aux_ref
  7.6 104.4 %shard_map.104 = (f32[8,1024]{1,0:T(8,128)}, f32[8,12]{1,0:T(8,128)}) custom-call(f32[4,12]{1,0:T(4,128)} %maximum_maximum_fusion.1.mode_ref, f32[16,128]{1,0:T(8,128)} %broadcast_in_dim.8.shift_ref, bf16[64,1024]{1,0:T(8,128)(2,1)} %u_ref.1, bf16[16,1024]{1,0:T(8,128)(2,1)} %maximum_maximum_fusion.aux_ref, bf16[8,64,768]{2,1,0:T(8,128)(2,1)} %table_ref.1, ...), custom_call_target="tpu_custom_call" | custom-call | tf_op jit(solution)/shard_map/pallas_call | solution.py:408
  112.1 0.0 copy-start.5
  112.1 1.4 %copy.17 = f32[8,1024]{1,0:T(8,128)} copy(f32[8,1024]{1,0:T(8,128)} %get-tuple-element.6) | data formatting | bytes 65536
  113.5 0.0 copy-done.5
  113.5 0.6 copy.18
  (7 shorter events, 0.0 us)
Async XLA Ops:
  0.6 0.8 copy-start
  3.0 0.7 copy-start.6
  3.7 0.7 copy-start.1
  4.3 0.8 copy-start.4
  5.3 0.8 copy-start.3
  6.1 0.8 copy-start.2
  112.1 1.4 %copy-start.5 = (f32[8,12]{1,0:T(8,128)S(1)}, f32[8,12]{1,0:T(8,128)}, u32[]{:S(2)}) copy-start(f32[8,12]{1,0:T(8,128)} %get-tuple-element.7) | copy-start | bytes 1156
